TPU v7x, 512 devices: a whole 4x4x16 slice. The times are simulated.
512 devices in a mesh: dom: 32 (over z_lo, y), feat: 16 (over z_hi, x, core).
Axes of the slice: x: 4, y: 4, z: 16 (z_hi: 2, z_lo: 8; z = z_hi * 8 + z_lo), core: 2. Of those that a mesh axis runs over, the one named last changes fastest.
Arguments:
- features: bfloat16 [512, 256, 128], P('dom', 'feat'), may hold values from -6 to 6
- tiles: bfloat16 [32, 32, 4, 128, 128], P('dom'), may hold values from 0 to 0.26, as said below
- block_rows: int32 [32, 32, 4], P('dom'), may hold values from 0 to 15, as said below
- block_cols: int32 [32, 32, 4], P('dom'), may hold values from 0 to 15
- block_counts: int32 [32, 32], P('dom'), may hold values from 1 to 4, as said below
- weight_one: bfloat16 [256, 256], replicated, may hold values from -0.375 to 0.375
- bias_one: float32 [256], replicated, may hold values from -3 to 3
- weight_two: bfloat16 [256, 256], replicated, may hold values from -0.375 to 0.375
- bias_two: float32 [256], replicated, may hold values from -3 to 3
Outputs:
- node_out: float32 [512, 256, 128], P('dom', 'feat')
Inputs may be any that keep to these rules, and one draw needn't show every extreme that they name: `tiles`: adjacency values are nonnegative. `block_rows`: within one pair of source and destination partitions the 4 slots name different row blocks. `block_counts`: slots at or past the count are not part of the operator. Each partition's pair with itself is full, and one destination partition is full from every source.
All inputs are finite; a program needn't handle non-finite values.
Results may differ from a plain program's by a relative error of at most 0.018.
Values may be sent and summed in bfloat16 or wider, within the bound.
No kernel may reach another device: no remote copies, remote signals or barrier semaphores. Data moves between devices by JAX's collectives and lax.ppermute only.
A program may use at most 64 MiB of HBM per device.

v0:
```python
import jax
import jax.numpy as jnp
from jax import lax
from jax.sharding import PartitionSpec as P


def slot_terms(source, tile_set, col_table, live_mask):
    selected = jnp.einsum(
        "pjb,bfk->pjfk", col_table, source, preferred_element_type=jnp.float32
    ).astype(jnp.bfloat16)
    products = jnp.einsum("pjfk,pjik->pjfi", selected, tile_set, preferred_element_type=jnp.float32)
    return jnp.where(live_mask[:, :, None, None], products, 0.0).astype(jnp.bfloat16)


def per_device(
    features,
    tiles,
    block_rows,
    block_cols,
    block_counts,
    weight_one,
    bias_one,
    weight_two,
    bias_two,
):
    tile_set = tiles[0]
    row_index = block_rows[0]
    col_index = block_cols[0]
    counts_here = block_counts[0]
    domains = lax.axis_size("dom")
    blocks_here = features.shape[0]
    slots = row_index.shape[1]
    live_mask = lax.broadcasted_iota(jnp.int32, (domains, slots), 1) < counts_here[:, None]
    block_iota = lax.broadcasted_iota(jnp.int32, (domains, slots, blocks_here), 2)
    col_table = (col_index[:, :, None] == block_iota).astype(jnp.bfloat16)
    row_table = (row_index[:, :, None] == block_iota).astype(jnp.bfloat16)

    def aggregate(source):
        terms = slot_terms(source, tile_set, col_table, live_mask)
        placed = jnp.einsum("pjr,pjfk->prfk", row_table, terms, preferred_element_type=jnp.float32)
        return lax.psum_scatter(
            placed.reshape(
                lax.axis_size("dom") * blocks_here, source.shape[1], source.shape[2]
            ).astype(jnp.bfloat16),
            "dom",
            scatter_dimension=0,
            tiled=True,
        )

    def transform(blocks, weight, bias_vector, last_layer):
        node_rows = lax.all_to_all(blocks, "feat", split_axis=0, concat_axis=1, tiled=True)
        result = jnp.einsum("bfk,fh->bhk", node_rows, weight, preferred_element_type=jnp.float32)
        result = result + bias_vector[None, :, None]
        if last_layer:
            return lax.all_to_all(
                result.astype(jnp.bfloat16), "feat", split_axis=1, concat_axis=0, tiled=True
            ).astype(result.dtype)
        return lax.all_to_all(
            jax.nn.relu(result).astype(jnp.bfloat16),
            "feat",
            split_axis=1,
            concat_axis=0,
            tiled=True,
        )

    hidden = transform(aggregate(features), weight_one, bias_one, False)
    return transform(aggregate(hidden), weight_two, bias_two, True)


def solution(mesh):
    placed = (
        P("dom", "feat", None),
        P("dom", None, None, None, None),
        P("dom", None, None),
        P("dom", None, None),
        P("dom", None),
        P(),
        P(),
        P(),
        P(),
    )
    return jax.shard_map(
        per_device, mesh=mesh, in_specs=placed, out_specs=P("dom", "feat", None), check_vma=False
    )
```

profile of v0, /device:TPU:1, one launch (start us, length us, event | category | flops | bytes accessed | tf_op | source)
XLA Modules:
  0.0 601.3 jit_solution(15495406895200002485)
XLA Ops:
  6.5 0.0 copy-start
  6.5 0.8 iota_compare_fusion.2
  7.3 0.8 copy.19
  8.1 1.2 convolution_convert_fusion.3
  9.3 4.5 fusion.13
  13.7 1.5 convolution_convert_fusion.1
  15.3 0.0 copy-start.2
  15.3 1.9 copy.23
  17.2 0.0 reduce-scatter.3.cloned.1.call-update
  17.2 0.0 reduce-scatter.5.cloned.1.call-start
  17.3 224.0 %reduce-scatter.3.cloned.1.call-done = bf16[16,16,128]{2,1,0:T(8,128)(2,1)} async-done(((bf16[512,16,128]{2,1,0:T(8,128)(2,1)}), bf16[16,16,128]{2,1,0:T(8,128)(2,1)}) %reduce-scatter.3.cloned.1.call-update) | async-done | bytes 65552 | tf_op jit(solution)/shard_map/reduce_scatter | solution.py:41
  241.2 46.7 %all_to_all.19 = bf16[16,16,128]{2,1,0:T(8,128)(2,1)S(1)} all-to-all(bf16[16,16,128]{2,1,0:T(8,128)(2,1)} %reduce-scatter.3.cloned.1.call-done), channel_id=1, replica_groups=mesh['dom'=32,'feat'=16] {'feat'}, dimensions={0} | all-to-all | bytes 131072 | tf_op jit(solution)/shard_map/all_to_all | solution.py:51
  288.0 0.2 fusion.20
  288.2 0.1 copy.24
  288.3 0.5 broadcast.22
  288.8 1.0 reduce
  289.8 17.4 %all_to_all.40 = bf16[16,2,1024]{2,1,0:T(2,128)(2,1)S(1)} all-to-all(bf16[16,2,1024]{2,1,0:T(2,128)(2,1)S(1)} %reshape.72), channel_id=1, replica_groups=mesh['dom'=32,'feat'=16] {'feat'}, dimensions={0} | all-to-all | bytes 131072 | tf_op jit(solution)/shard_map/all_to_all | solution.py:58
  307.3 0.1 reshape.73
  307.4 0.0 copy-done.2
  307.4 0.3 convolution_convert_fusion.2
  307.7 4.5 fusion.10
  312.2 1.5 convolution_convert_fusion
  313.7 1.9 copy.28
  315.6 0.0 reduce-scatter.5.cloned.1.call-update
  315.7 211.7 %reduce-scatter.5.cloned.1.call-done = bf16[16,16,128]{2,1,0:T(8,128)(2,1)} async-done(((bf16[512,16,128]{2,1,0:T(8,128)(2,1)}), bf16[16,16,128]{2,1,0:T(8,128)(2,1)}) %reduce-scatter.5.cloned.1.call-update) | async-done | bytes 65552 | tf_op jit(solution)/shard_map/reduce_scatter | solution.py:41
  527.4 47.5 %all_to_all.41 = bf16[16,16,128]{2,1,0:T(8,128)(2,1)S(1)} all-to-all(bf16[16,16,128]{2,1,0:T(8,128)(2,1)} %reduce-scatter.5.cloned.1.call-done), channel_id=1, replica_groups=mesh['dom'=32,'feat'=16] {'feat'}, dimensions={0} | all-to-all | bytes 131072 | tf_op jit(solution)/shard_map/all_to_all | solution.py:51
  574.9 0.2 fusion.19
  575.1 0.1 copy.29
  575.3 1.0 reduce.1
  576.3 17.4 %all_to_all.42 = bf16[16,2,1024]{2,1,0:T(2,128)(2,1)S(1)} all-to-all(bf16[16,2,1024]{2,1,0:T(2,128)(2,1)S(1)} %reshape.74), channel_id=1, replica_groups=mesh['dom'=32,'feat'=16] {'feat'}, dimensions={0} | all-to-all | bytes 131072 | tf_op jit(solution)/shard_map/all_to_all | solution.py:55
  593.7 0.1 reshape.75
  593.8 0.7 convert.1
  (12 shorter events, 0.1 us)
Async XLA Ops:
  6.5 281.4 %copy-start = (bf16[256,256]{1,0:T(8,128)(2,1)S(1)}, bf16[256,256]{1,0:T(8,128)(2,1)}, u32[]{:S(2)}) copy-start(bf16[256,256]{1,0:T(8,128)(2,1)} %param.14) | copy-start | bytes 393220
  6.5 234.7 %reduce-scatter.3.cloned.1.call-start = ((), (), s32[]{:S(2)}) async-start(), calls=%async_computation.6 | async-start | bytes 2162688 | tf_op jit(solution)/shard_map/reduce_scatter | solution.py:41
  13.7 274.2 %copy-start.3 = (f32[256]{0:T(256)S(1)}, f32[256]{0:T(256)}, u32[]{:S(2)}) copy-start(f32[256]{0:T(256)} %param.15) | copy-start | bytes 3076
  15.3 292.1 %copy-start.2 = (s32[1,32,4]{1,2,0:T(4,128)S(1)}, s32[1,32,4]{1,2,0:T(4,128)}, u32[]{:S(2)}) copy-start(s32[1,32,4]{1,2,0:T(4,128)} %param.12) | copy-start | bytes 1540
  17.2 510.2 %reduce-scatter.5.cloned.1.call-start = ((), (), s32[]{:S(2)}) async-start(), calls=%async_computation.7 | async-start | bytes 2162688 | tf_op jit(solution)/shard_map/reduce_scatter | solution.py:41
  312.2 262.7 %copy-start.1 = (bf16[256,256]{1,0:T(8,128)(2,1)S(1)}, bf16[256,256]{1,0:T(8,128)(2,1)}, u32[]{:S(2)}) copy-start(bf16[256,256]{1,0:T(8,128)(2,1)} %param.16) | copy-start | bytes 393220
  312.2 262.7 %copy-start.4 = (f32[256]{0:T(256)S(1)}, f32[256]{0:T(256)}, u32[]{:S(2)}) copy-start(f32[256]{0:T(256)} %param.17) | copy-start | bytes 3076
Sparse Core Ops, SparseCore 0:
  17.3 223.8 reduce-scatter.2
  315.8 211.5 reduce-scatter.4
where the time goes:
time: 602 us; the launch traced here: 601 us
  waiting for transfers between devices  436 us (72%)
  blocking collectives  129 us (21%)
  matrix products  13.9 us (2%)
  between operations  13.5 us (2%)
    reduce_scatter x2, waiting for transfers between devices, aggregate(): lax.psum_scatter(placed.reshape(lax.axis_size('dom') * blocks_here, sourc...  436 us
    all_to_all x2, blocking collectives, transform(): lax.all_to_all(blocks, 'feat', split_axis=0, concat_axis=1, tiled=True)  94.2 us
    all_to_all x1, blocking collectives, transform(): lax.all_to_all(jax.nn.relu(result).astype(jnp.bfloat16), 'feat', split_ax...  17.4 us
    all_to_all x1, blocking collectives, transform(): lax.all_to_all(result.astype(jnp.bfloat16), 'feat', split_axis=1, concat_...  17.4 us
  transfers between devices with their start and end apart: 2, of which 2 were waited for; matrix products, arithmetic and copies ran while one was open for 0% of the time, Pallas kernels for 0%

commit v1 on v0

v1 whole, which is shorter than its diff:
```python
import functools

import jax
import jax.numpy as jnp
from jax import lax
from jax.experimental import pallas as pl
from jax.experimental.pallas import tpu as pltpu
from jax.sharding import Mesh
from jax.sharding import PartitionSpec as P

QUADS, ZQ, YS, HS, XC = 2, 4, 4, 2, 8
CAP, BLK, FW, ROWS = 4, 128, 16, 16
MSG = CAP * FW
META = 8
BF, F32 = jnp.bfloat16, jnp.float32
VMEM = pl.BlockSpec(memory_space=pltpu.VMEM)
NT = (((1,), (1,)), ((), ()))
TN = (((0,), (0,)), ((), ()))


def terms_kernel(with_meta, q_ref, cols_ref, counts_ref, rows_ref, v_ref, tile_ref, out_ref):
    first = ((pl.program_id(0) ^ q_ref[0]) * ZQ + pl.program_id(1)) * YS
    for y in range(YS):
        p = first + y
        count = counts_ref[0, p]
        for j in range(CAP):
            block = v_ref[cols_ref[0, p, j]]
            term = lax.dot_general(block, tile_ref[0, y, j], NT, preferred_element_type=F32)
            term = jnp.where(j < count, term, 0.0).astype(BF)
            out_ref[0, y, 0, j * FW : (j + 1) * FW, :] = term
        if with_meta:
            lane = lax.broadcasted_iota(jnp.int32, (META, BLK), 1)
            slot = (lane // FW) % CAP
            place = lane % FW
            for j in range(CAP):
                place = jnp.where(slot == j, place + rows_ref[0, p, j] * FW, place)
            out_ref[0, y, 0, MSG:, :] = place.astype(F32).astype(BF)


def slot_terms(q, cols, counts, rows, values, tiles, with_meta):
    lines = MSG + META if with_meta else MSG
    msg = pl.pallas_call(
        functools.partial(terms_kernel, with_meta),
        grid_spec=pltpu.PrefetchScalarGridSpec(
            num_scalar_prefetch=4,
            grid=(QUADS, ZQ),
            in_specs=[
                pl.BlockSpec((ROWS, FW, BLK), lambda r, b, *_: (0, 0, 0)),
                pl.BlockSpec((1, YS, CAP, BLK, BLK), lambda r, b, q, *_: (0, (r ^ q[0]) * ZQ + b, 0, 0, 0)),
            ],
            out_specs=pl.BlockSpec((1, YS, 1, lines, BLK), lambda r, b, *_: (b, 0, r, 0, 0)),
        ),
        out_shape=jax.ShapeDtypeStruct((ZQ, YS, QUADS, lines, BLK), BF),
        compiler_params=pltpu.CompilerParams(vmem_limit_bytes=16 << 20),
        name="slot_terms",
    )(q, cols, counts, rows, values, tiles)
    return msg.reshape(ZQ * YS, QUADS * lines, BLK)


def placed_sum(msg_of, meta_of):
    total = jnp.zeros((ROWS * FW, BLK), F32)
    lane = lax.broadcasted_iota(jnp.int32, (META, BLK), 1)
    spot = lax.broadcasted_iota(jnp.int32, (ROWS * FW, BLK), 0).astype(F32)
    for s in range(0, ZQ * YS, 4):
        halves = []
        for t in (s, s + 2):
            place = jnp.where(lane < MSG, meta_of(t).astype(F32), meta_of(t + 1).astype(F32))
            place = jnp.concatenate([place] * (ROWS * FW // META), axis=0)
            halves.append(jnp.where(spot == place, 1.0, 0.0).astype(BF))
        put = jnp.concatenate(halves, axis=1)
        lines = jnp.concatenate([msg_of(s + i) for i in range(4)], axis=0)
        total += jnp.dot(put, lines, preferred_element_type=F32)
    return total


def first_sum_kernel(q_ref, msg_ref, out_ref):
    for r in range(QUADS):
        base = r * (MSG + META)
        total = placed_sum(
            lambda s: msg_ref[s, base : base + MSG, :],
            lambda s: msg_ref[s, base + MSG : base + MSG + META, :],
        ).astype(BF)
        for h in range(HS):
            out_ref[r ^ q_ref[0], h] = total


def second_sum_kernel(r, msg_ref, meta_ref, *refs):
    base = r * (MSG + META)
    total = placed_sum(
        lambda s: msg_ref[s, r * MSG : (r + 1) * MSG, :],
        lambda s: meta_ref[s, base + MSG : base + MSG + META, :],
    )
    if len(refs) == 2:
        bias_ref, out_ref = refs
        out_ref[...] = total + bias_ref[...]
    else:
        refs[0][...] = total.astype(BF)


def dense_kernel(agg_ref, w1_ref, b1_ref, w2_ref, out_ref):
    half = agg_ref.shape[0] // 2
    agg = agg_ref[:half].astype(F32) + agg_ref[half:].astype(F32)
    agg = jnp.concatenate([agg[:, i * FW : (i + 1) * FW, :].reshape(half * FW, BLK) for i in range(2)], axis=1)
    hidden = lax.dot_general(w1_ref[...], agg.astype(BF), TN, preferred_element_type=F32)
    hidden = jnp.maximum(hidden + b1_ref[...], 0.0).astype(BF)
    out = lax.dot_general(w2_ref[...], hidden, TN, preferred_element_type=F32).astype(BF)
    for i in range(2):
        out_ref[:, i] = out[:, i * BLK : (i + 1) * BLK].reshape(XC, FW, BLK)


def per_device(features, tiles, rows, cols, counts, w1, b1, w2, b2):
    q = lax.axis_index("q").astype(jnp.int32).reshape(1)
    h = lax.axis_index("h")
    w2_half = lax.dynamic_slice_in_dim(w2, h * (XC * FW), XC * FW, 1)
    b1_wide = jnp.broadcast_to(b1[:, None], (b1.shape[0], 2 * BLK))
    own = lax.axis_index(("h", "x", "c")) * FW
    b2_wide = jnp.broadcast_to(lax.dynamic_slice_in_dim(b2, own, FW)[None, :, None], (ROWS, FW, BLK))
    b2_wide = b2_wide.reshape(ROWS * FW, BLK)

    def quad_exchange(msg):
        return lax.all_to_all(msg, ("b", "y"), 0, 0, tiled=True)

    msg1 = quad_exchange(slot_terms(q, cols, counts, rows, features, tiles, True))
    sums = pl.pallas_call(
        first_sum_kernel,
        in_specs=[pl.BlockSpec(memory_space=pltpu.SMEM), VMEM],
        out_specs=VMEM,
        out_shape=jax.ShapeDtypeStruct((QUADS, HS, ROWS * FW, BLK), BF),
        name="first_sum",
    )(q, msg1)
    sums = sums.reshape(QUADS * HS * XC, 2 * FW, BLK)
    sums = lax.all_to_all(sums, ("q", "h", "x", "c"), 0, 0, tiled=True)
    z = pl.pallas_call(
        dense_kernel,
        in_specs=[VMEM] * 4,
        out_specs=VMEM,
        out_shape=jax.ShapeDtypeStruct((XC, 2, FW, BLK), BF),
        name="dense",
    )(sums, w1, b1_wide, w2_half)
    z = lax.all_to_all(z, ("x", "c"), 0, 0, tiled=True).reshape(ROWS, FW, BLK)

    msg2 = quad_exchange(slot_terms(q, cols, counts, rows, z, tiles, False))
    far = pl.pallas_call(
        functools.partial(second_sum_kernel, 1),
        in_specs=[VMEM] * 2,
        out_specs=VMEM,
        out_shape=jax.ShapeDtypeStruct((ROWS * FW, BLK), BF),
        name="far_sum",
    )(msg2, msg1)
    far = lax.ppermute(far, "q", [(0, 1), (1, 0)])
    near = pl.pallas_call(
        functools.partial(second_sum_kernel, 0),
        in_specs=[VMEM] * 3,
        out_specs=VMEM,
        out_shape=jax.ShapeDtypeStruct((ROWS * FW, BLK), F32),
        name="near_sum",
    )(msg2, msg1, b2_wide)
    return (near + far.astype(F32)).reshape(ROWS, FW, BLK)


def solution(mesh):
    fine = Mesh(mesh.devices.reshape(QUADS, ZQ, YS, HS, 4, 2), ("q", "b", "y", "h", "x", "c"))
    dom, feat = ("q", "b", "y"), ("h", "x", "c")
    placed = (
        P(dom, feat, None),
        P(dom, None, None, None, None),
        P(dom, None, None),
        P(dom, None, None),
        P(dom, None),
        P(),
        P(),
        P(),
        P(),
    )
    return jax.shard_map(
        per_device, mesh=fine, in_specs=placed, out_specs=P(dom, feat, None), check_vma=False
    )
```

time: 602 us -> 130 us (0.22)
  the two profiles are of different devices: /device:TPU:1 before, /device:TPU:2 now
where the time goes in v1:
time: 130 us; the launch traced here: 129 us
  blocking collectives  56.6 us (44%)
  waiting for transfers between devices  24.8 us (19%)
  starting transfers between devices  19.1 us (15%)
  Pallas kernels  17.2 us (13%)
  local copies, waits for them, and re-layouts  9.84 us (8%)
  other arithmetic  1.57 us (1%)
    all_to_all x2, blocking collectives, quad_exchange(): return lax.all_to_all(msg, ('b', 'y'), 0, 0, tiled=True)  48.3 us
    all_to_all x1, waiting for transfers between devices, per_device(): sums = lax.all_to_all(sums, ('q', 'h', 'x', 'c'), 0, 0, tiled=True)  18.7 us
    all_to_all x1, starting transfers between devices, per_device(): sums = lax.all_to_all(sums, ('q', 'h', 'x', 'c'), 0, 0, tiled=True)  15.5 us
    pallas_call x2, Pallas kernels, slot_terms(): pl.pallas_call(functools.partial(terms_kernel, with_meta), grid_spec=pltp...  8.58 us
    all_to_all x1, blocking collectives, per_device(): z = lax.all_to_all(z, ('x', 'c'), 0, 0, tiled=True).reshape(ROWS, FW, BLK)  8.33 us
    unnamed x20, local copies, waits for them, and re-layouts  7.45 us
    ppermute x1, waiting for transfers between devices, per_device(): far = lax.ppermute(far, 'q', [(0, 1), (1, 0)])  6.07 us
    ppermute x1, starting transfers between devices, per_device(): far = lax.ppermute(far, 'q', [(0, 1), (1, 0)])  3.55 us
  transfers between devices with their start and end apart: 2, of which 2 were waited for; matrix products, arithmetic and copies ran while one was open for 1% of the time, Pallas kernels for 2%

profile of v1, /device:TPU:2, one launch (start us, length us, event | category | flops | bytes accessed | tf_op | source)
XLA Modules:
  0.0 129.2 jit_solution(2534990709147657968)
XLA Ops:
  0.0 0.0 copy-start
  0.0 0.8 copy.12.cols_ref
  0.8 0.8 copy.13.rows_ref
  1.6 2.2 %copy-done.1 = bf16[1,32,4,128,128]{4,3,2,1,0:T(8,128)(2,1)S(1)} copy-done((bf16[1,32,4,128,128]{4,3,2,1,0:T(8,128)(2,1)S(1)}, bf16[1,32,4,128,128]{4,3,2,1,0:T(8,128)(2,1)}, u32[]{:S(2)}) %copy-start.1) | copy-done | bytes 4194328
  3.8 0.8 copy-done.3
  4.6 0.7 copy-done.4
  5.3 4.3 %slot_terms.2 = bf16[4,4,2,72,128]{4,3,2,1,0:T(8,128)(2,1)S(1)} custom-call(s32[1]{0:T(128)} %bitcast.q_ref, s32[1,32,4]{2,1,0:T(8,128)S(1)} %copy.12.cols_ref, s32[1,32]{1,0:T(1,128)S(1)} %copy-done.4, s32[1,32,4]{2,1,0:T(8,128)S(1)} %copy.13.rows_ref, bf16[16,16,128]{2,1,0:T(8,128)(2,1)S(1)} %copy-done.3, bf16[1,32,4,128,128]{4,3,2,1,0:T(8,128)(2,1)S(1)} %copy-done.1), custom_call_target="tpu_custom_call" | custom-call | tf_op jit(solution)/shard_map/slot_terms/pallas_call | solution.py:42
  9.6 26.4 %all_to_all.20.msg_ref.meta_ref = bf16[16,144,128]{2,1,0:T(8,128)(2,1)} all-to-all(bf16[16,144,128]{2,1,0:T(8,128)(2,1)S(1)} %bitcast.6), channel_id=1, replica_groups=mesh['q'=2,'b'=4,'y'=4,'h'=2,'x'=4,'c'=2] {'b','y'}, dimensions={0} | all-to-all | bytes 1179648 | tf_op jit(solution)/shard_map/all_to_all | solution.py:121
  36.0 2.2 %first_sum.1 = bf16[2,2,256,128]{3,2,1,0:T(8,128)(2,1)} custom-call(s32[1]{0:T(128)} %bitcast.q_ref, bf16[16,144,128]{2,1,0:T(8,128)(2,1)} %all_to_all.20.msg_ref.meta_ref), custom_call_target="tpu_custom_call" | custom-call | tf_op jit(solution)/shard_map/first_sum/pallas_call | solution.py:124
  38.2 15.5 %all-to-all-start.1 = ((bf16[32,32,128]{2,1,0:T(8,128)(2,1)}), bf16[32,32,128]{2,1,0:T(8,128)(2,1)S(1)}, u32[]{:S(2)}, u32[]{:S(2)}) async-start(bf16[32,32,128]{2,1,0:T(8,128)(2,1)} %bitcast.9), calls=%async_computation.1 | async-start | bytes 524288 | tf_op jit(solution)/shard_map/all_to_all | solution.py:132
  53.8 0.0 copy-done
  53.8 0.0 copy-start.8
  53.8 0.6 constant_dynamic-slice_fusion.w2_ref
  54.4 18.7 %all-to-all-done.1.agg_ref = bf16[32,32,128]{2,1,0:T(8,128)(2,1)S(1)} async-done(((bf16[32,32,128]{2,1,0:T(8,128)(2,1)}), bf16[32,32,128]{2,1,0:T(8,128)(2,1)S(1)}, u32[]{:S(2)}, u32[]{:S(2)}) %all-to-all-start.1) | async-done | bytes 262176 | tf_op jit(solution)/shard_map/all_to_all | solution.py:132
  73.2 0.0 copy-done.7
  73.2 0.8 broadcast_in_dim.16.b1_ref
  74.0 0.0 copy-done.6
  74.0 2.1 %dense.1 = bf16[8,2,16,128]{3,2,1,0:T(8,128)(2,1)} custom-call(bf16[32,32,128]{2,1,0:T(8,128)(2,1)} %copy-done.6, bf16[256,256]{1,0:T(8,128)(2,1)} %w1_ref.1, f32[256,256]{1,0:T(8,128)} %broadcast_in_dim.16.b1_ref, bf16[256,128]{1,0:T(8,128)(2,1)} %constant_dynamic-slice_fusion.w2_ref), custom_call_target="tpu_custom_call" | custom-call | tf_op jit(solution)/shard_map/dense/pallas_call | solution.py:133
  76.1 8.3 %all_to_all.21 = bf16[8,2,16,128]{3,2,1,0:T(8,128)(2,1)S(1)} all-to-all(bf16[8,2,16,128]{3,2,1,0:T(8,128)(2,1)} %dense.1), channel_id=1, replica_groups=mesh['q'=2,'b'=4,'y'=4,'h'=2,'x'=4,'c'=2] {'x','c'}, dimensions={0} | all-to-all | bytes 131072 | tf_op jit(solution)/shard_map/all_to_all | solution.py:140
  84.4 0.0 copy-done.5
  84.4 2.2 %copy-done.2 = bf16[1,32,4,128,128]{4,3,2,1,0:T(8,128)(2,1)S(1)} copy-done((bf16[1,32,4,128,128]{4,3,2,1,0:T(8,128)(2,1)S(1)}, bf16[1,32,4,128,128]{4,3,2,1,0:T(8,128)(2,1)}, u32[]{:S(2)}) %copy-start.2) | copy-done | bytes 4194328
  86.6 4.3 %slot_terms.3 = bf16[4,4,2,64,128]{4,3,2,1,0:T(8,128)(2,1)S(1)} custom-call(s32[1]{0:T(128)} %bitcast.q_ref, s32[1,32,4]{2,1,0:T(8,128)S(1)} %copy.12.cols_ref, s32[1,32]{1,0:T(1,128)S(1)} %copy-done.5, s32[1,32,4]{2,1,0:T(8,128)S(1)} %copy.13.rows_ref, bf16[16,16,128]{2,1,0:T(8,128)(2,1)S(1)} %bitcast.8, bf16[1,32,4,128,128]{4,3,2,1,0:T(8,128)(2,1)S(1)} %copy-done.2), custom_call_target="tpu_custom_call" | custom-call | tf_op jit(solution)/shard_map/slot_terms/pallas_call | solution.py:42
  90.9 21.8 %all_to_all.22.msg_ref = bf16[16,128,128]{2,1,0:T(8,128)(2,1)} all-to-all(bf16[16,128,128]{2,1,0:T(8,128)(2,1)S(1)} %bitcast.7), channel_id=1, replica_groups=mesh['q'=2,'b'=4,'y'=4,'h'=2,'x'=4,'c'=2] {'b','y'}, dimensions={0} | all-to-all | bytes 1048576 | tf_op jit(solution)/shard_map/all_to_all | solution.py:121
  112.7 2.1 %far_sum.1 = bf16[256,128]{1,0:T(8,128)(2,1)} custom-call(bf16[16,128,128]{2,1,0:T(8,128)(2,1)} %all_to_all.22.msg_ref, bf16[16,144,128]{2,1,0:T(8,128)(2,1)} %all_to_all.20.msg_ref.meta_ref), custom_call_target="tpu_custom_call" | custom-call | tf_op jit(solution)/shard_map/far_sum/pallas_call | solution.py:143
  114.9 3.5 %collective-permute-start = (bf16[256,128]{1,0:T(8,128)(2,1)}, bf16[256,128]{1,0:T(8,128)(2,1)S(1)}, u32[]{:S(2)}, u32[]{:S(2)}) collective-permute-start(bf16[256,128]{1,0:T(8,128)(2,1)} %far_sum.1), channel_id=1, source_target_pairs={{0,256},{256,0},{1,257},{257,1},{2,258},{258,2},{3,259},{259,3},{4... | collective-permute-start | bytes 196616 | tf_op jit(solution)/shard_map/ppermute | solution.py:150
  118.4 0.0 copy-done.8
  118.4 0.1 dynamic_slice.7
  118.5 0.1 broadcast_in_dim.18
  118.6 0.8 broadcast_in_dim.19.refs_0_
  119.4 2.2 %near_sum.1 = f32[256,128]{1,0:T(8,128)} custom-call(bf16[16,128,128]{2,1,0:T(8,128)(2,1)} %all_to_all.22.msg_ref, bf16[16,144,128]{2,1,0:T(8,128)(2,1)} %all_to_all.20.msg_ref.meta_ref, f32[256,128]{1,0:T(8,128)} %broadcast_in_dim.19.refs_0_), custom_call_target="tpu_custom_call" | custom-call | tf_op jit(solution)/shard_map/near_sum/pallas_call | solution.py:151
  121.6 6.1 %collective-permute-done = bf16[256,128]{1,0:T(8,128)(2,1)S(1)} collective-permute-done((bf16[256,128]{1,0:T(8,128)(2,1)}, bf16[256,128]{1,0:T(8,128)(2,1)S(1)}, u32[]{:S(2)}, u32[]{:S(2)}) %collective-permute-start) | collective-permute-done | bytes 65568 | tf_op jit(solution)/shard_map/ppermute | solution.py:150
  127.6 1.6 %convert_add_fusion = f32[256,128]{1,0:T(8,128)} fusion(f32[256,128]{1,0:T(8,128)} %near_sum.1, bf16[256,128]{1,0:T(8,128)(2,1)S(1)} %collective-permute-done), kind=kLoop, calls=%fused_computation | loop fusion | flops 65536 | bytes 327680 | tf_op jit(solution)/shard_map/add | solution.py:158
  (8 shorter events, 0.0 us)
Async XLA Ops:
  0.0 53.8 %copy-start = (bf16[256,256]{1,0:T(8,128)(2,1)S(1)}, bf16[256,256]{1,0:T(8,128)(2,1)}, u32[]{:S(2)}) copy-start(bf16[256,256]{1,0:T(8,128)(2,1)} %param.16) | copy-start | bytes 393220
  0.0 73.2 %copy-start.7 = (f32[256]{0:T(256)S(1)}, f32[256]{0:T(256)}, u32[]{:S(2)}) copy-start(f32[256]{0:T(256)} %param.15) | copy-start | bytes 3076
  1.6 2.2 %copy-start.1 = (bf16[1,32,4,128,128]{4,3,2,1,0:T(8,128)(2,1)S(1)}, bf16[1,32,4,128,128]{4,3,2,1,0:T(8,128)(2,1)}, u32[]{:S(2)}) copy-start(bf16[1,32,4,128,128]{4,3,2,1,0:T(8,128)(2,1)} %tile_ref.3) | copy-start | bytes 12582916
  3.8 0.8 copy-start.3
  4.6 0.7 copy-start.4
  5.2 79.2 %copy-start.5 = (s32[1,32]{1,0:T(1,128)S(1)}, s32[1,32]{1,0:T(1,128)}, u32[]{:S(2)}) copy-start(s32[1,32]{1,0:T(1,128)} %counts_ref.3) | copy-start | bytes 388
  38.2 35.0 %all-to-all-start.1 = ((bf16[32,32,128]{2,1,0:T(8,128)(2,1)}), bf16[32,32,128]{2,1,0:T(8,128)(2,1)S(1)}, u32[]{:S(2)}, u32[]{:S(2)}) async-start(bf16[32,32,128]{2,1,0:T(8,128)(2,1)} %bitcast.9), calls=%async_computation.1 | async-start | bytes 524288 | tf_op jit(solution)/shard_map/all_to_all | solution.py:132
  53.8 64.7 %copy-start.8 = (f32[256]{0:T(256)S(1)}, f32[256]{0:T(256)}, u32[]{:S(2)}) copy-start(f32[256]{0:T(256)} %param.17) | copy-start | bytes 3076
  73.2 0.8 copy-start.6
  84.4 2.2 %copy-start.2 = (bf16[1,32,4,128,128]{4,3,2,1,0:T(8,128)(2,1)S(1)}, bf16[1,32,4,128,128]{4,3,2,1,0:T(8,128)(2,1)}, u32[]{:S(2)}) copy-start(bf16[1,32,4,128,128]{4,3,2,1,0:T(8,128)(2,1)} %tile_ref.3) | copy-start | bytes 12582916
  114.9 12.8 %collective-permute-start = (bf16[256,128]{1,0:T(8,128)(2,1)}, bf16[256,128]{1,0:T(8,128)(2,1)S(1)}, u32[]{:S(2)}, u32[]{:S(2)}) collective-permute-start(bf16[256,128]{1,0:T(8,128)(2,1)} %far_sum.1), channel_id=1, source_target_pairs={{0,256},{256,0},{1,257},{257,1},{2,258},{258,2},{3,259},{259,3},{4... | collective-permute-start | bytes 196616 | tf_op jit(solution)/shard_map/ppermute | solution.py:150

commit v2 on v1

--- a/solution.py
+++ b/solution.py
@@ -12,49 +12,78 @@
 CAP, BLK, FW, ROWS = 4, 128, 16, 16
 MSG = CAP * FW
 META = 8
+ROOM = pltpu.CompilerParams(vmem_limit_bytes=8 << 20)
 BF, F32 = jnp.bfloat16, jnp.float32
 VMEM = pl.BlockSpec(memory_space=pltpu.VMEM)
 NT = (((1,), (1,)), ((), ()))
 TN = (((0,), (0,)), ((), ()))
 
 
-def terms_kernel(with_meta, q_ref, cols_ref, counts_ref, rows_ref, v_ref, tile_ref, out_ref):
-    first = ((pl.program_id(0) ^ q_ref[0]) * ZQ + pl.program_id(1)) * YS
-    for y in range(YS):
-        p = first + y
-        count = counts_ref[0, p]
-        for j in range(CAP):
-            block = v_ref[cols_ref[0, p, j]]
-            term = lax.dot_general(block, tile_ref[0, y, j], NT, preferred_element_type=F32)
-            term = jnp.where(j < count, term, 0.0).astype(BF)
-            out_ref[0, y, 0, j * FW : (j + 1) * FW, :] = term
-        if with_meta:
-            lane = lax.broadcasted_iota(jnp.int32, (META, BLK), 1)
-            slot = (lane // FW) % CAP
-            place = lane % FW
-            for j in range(CAP):
-                place = jnp.where(slot == j, place + rows_ref[0, p, j] * FW, place)
-            out_ref[0, y, 0, MSG:, :] = place.astype(F32).astype(BF)
-
-
-def slot_terms(q, cols, counts, rows, values, tiles, with_meta):
+def terms_kernel(with_meta, *refs):
+    tables, v_ref, tile_ref, out_ref = refs[: 2 + with_meta], *refs[2 + with_meta : 5 + with_meta]
+    held, v_held, tile_held, sems = refs[5 + with_meta : -3], *refs[-3:]
+    q = lax.axis_index("q").astype(jnp.int32)
+
+    def first_of(step):
+        return ((step // ZQ ^ q) * ZQ + step % ZQ) * YS
+
+    small = list(zip((*tables, v_ref), (*held, v_held)))
+    copies = [pltpu.make_async_copy(src, dst, sems.at[i]) for i, (src, dst) in enumerate(small)]
+    for step in range(QUADS * ZQ):
+        chunk = tile_ref.at[0, pl.ds(first_of(step), YS)]
+        copies.append(pltpu.make_async_copy(chunk, tile_held.at[step], sems.at[len(copies)]))
+    for copy in copies:
+        copy.start()
+    for copy in copies[: len(small)]:
+        copy.wait()
+    cols_ref, counts_ref = held[:2]
+    for step in range(QUADS * ZQ):
+        copies[len(small) + step].wait()
+        for y in range(YS):
+            p = first_of(step) + y
+            count = counts_ref[0, p]
+            at = (y, step % ZQ, step // ZQ)
+            for j in range(0, CAP, 2):
+                pair = jnp.concatenate([v_held[cols_ref[0, j + i, p]] for i in range(2)], axis=0)
+                tiles = tile_held[step, y, j : j + 2].reshape(2 * BLK, BLK)
+                term = lax.dot_general(pair, tiles, NT, preferred_element_type=F32)
+                for i in range(2):
+                    mine = term[i * FW : (i + 1) * FW, i * BLK : (i + 1) * BLK]
+                    mine = jnp.where(j + i < count, mine, 0.0).astype(BF)
+                    out_ref[*at, (j + i) * FW : (j + i + 1) * FW, :] = mine
+            if with_meta:
+                lane = lax.broadcasted_iota(jnp.int32, (META, BLK), 1)
+                slot = (lane // FW) % CAP
+                place = lane % FW
+                for j in range(CAP):
+                    place = jnp.where(slot == j, place + held[2][0, j, p] * FW, place)
+                out_ref[*at, MSG:, :] = place.astype(F32).astype(BF)
+
+
+def slot_terms(tables, values, tiles):
+    with_meta = len(tables) == 3
     lines = MSG + META if with_meta else MSG
+    steps = QUADS * ZQ
+    hbm = pl.BlockSpec(memory_space=pltpu.HBM)
     msg = pl.pallas_call(
         functools.partial(terms_kernel, with_meta),
-        grid_spec=pltpu.PrefetchScalarGridSpec(
-            num_scalar_prefetch=4,
-            grid=(QUADS, ZQ),
-            in_specs=[
-                pl.BlockSpec((ROWS, FW, BLK), lambda r, b, *_: (0, 0, 0)),
-                pl.BlockSpec((1, YS, CAP, BLK, BLK), lambda r, b, q, *_: (0, (r ^ q[0]) * ZQ + b, 0, 0, 0)),
-            ],
-            out_specs=pl.BlockSpec((1, YS, 1, lines, BLK), lambda r, b, *_: (b, 0, r, 0, 0)),
-        ),
-        out_shape=jax.ShapeDtypeStruct((ZQ, YS, QUADS, lines, BLK), BF),
-        compiler_params=pltpu.CompilerParams(vmem_limit_bytes=16 << 20),
+        in_specs=[hbm] * len(tables) + [pl.BlockSpec(memory_space=pl.ANY), hbm],
+        out_specs=VMEM,
+        out_shape=jax.ShapeDtypeStruct((YS, ZQ, QUADS, lines, BLK), BF),
+        scratch_shapes=[pltpu.SMEM(table.shape, table.dtype) for table in tables]
+        + [
+            pltpu.VMEM(values.shape, values.dtype),
+            pltpu.VMEM((steps, YS, CAP, BLK, BLK), BF),
+            pltpu.SemaphoreType.DMA((len(tables) + 1 + steps,)),
+        ],
+        compiler_params=ROOM,
         name="slot_terms",
-    )(q, cols, counts, rows, values, tiles)
-    return msg.reshape(ZQ * YS, QUADS * lines, BLK)
+    )(*tables, values, tiles)
+    return msg.reshape(YS * ZQ, QUADS * lines, BLK)
+
+
+def in_hbm(array):
+    return pltpu.with_memory_space_constraint(array, pltpu.HBM)
 
 
 def placed_sum(msg_of, meta_of):
@@ -102,7 +131,8 @@
     agg = agg_ref[:half].astype(F32) + agg_ref[half:].astype(F32)
     agg = jnp.concatenate([agg[:, i * FW : (i + 1) * FW, :].reshape(half * FW, BLK) for i in range(2)], axis=1)
     hidden = lax.dot_general(w1_ref[...], agg.astype(BF), TN, preferred_element_type=F32)
-    hidden = jnp.maximum(hidden + b1_ref[...], 0.0).astype(BF)
+    bias = jnp.transpose(jnp.broadcast_to(b1_ref[...], (BLK, b1_ref.shape[1])))
+    hidden = jnp.maximum(hidden + jnp.concatenate([bias, bias], axis=1), 0.0).astype(BF)
     out = lax.dot_general(w2_ref[...], hidden, TN, preferred_element_type=F32).astype(BF)
     for i in range(2):
         out_ref[:, i] = out[:, i * BLK : (i + 1) * BLK].reshape(XC, FW, BLK)
@@ -112,20 +142,22 @@
     q = lax.axis_index("q").astype(jnp.int32).reshape(1)
     h = lax.axis_index("h")
     w2_half = lax.dynamic_slice_in_dim(w2, h * (XC * FW), XC * FW, 1)
-    b1_wide = jnp.broadcast_to(b1[:, None], (b1.shape[0], 2 * BLK))
+    cols, rows = (jnp.swapaxes(table, 1, 2) for table in (cols, rows))
+    cols, rows, counts, features, tiles = (in_hbm(array) for array in (cols, rows, counts, features, tiles))
     own = lax.axis_index(("h", "x", "c")) * FW
     b2_wide = jnp.broadcast_to(lax.dynamic_slice_in_dim(b2, own, FW)[None, :, None], (ROWS, FW, BLK))
     b2_wide = b2_wide.reshape(ROWS * FW, BLK)
 
     def quad_exchange(msg):
-        return lax.all_to_all(msg, ("b", "y"), 0, 0, tiled=True)
-
-    msg1 = quad_exchange(slot_terms(q, cols, counts, rows, features, tiles, True))
+        return lax.all_to_all(msg, ("y", "b"), 0, 0, tiled=True)
+
+    msg1 = quad_exchange(slot_terms((cols, counts, rows), features, tiles))
     sums = pl.pallas_call(
         first_sum_kernel,
         in_specs=[pl.BlockSpec(memory_space=pltpu.SMEM), VMEM],
         out_specs=VMEM,
         out_shape=jax.ShapeDtypeStruct((QUADS, HS, ROWS * FW, BLK), BF),
+        compiler_params=ROOM,
         name="first_sum",
     )(q, msg1)
     sums = sums.reshape(QUADS * HS * XC, 2 * FW, BLK)
@@ -135,16 +167,18 @@
         in_specs=[VMEM] * 4,
         out_specs=VMEM,
         out_shape=jax.ShapeDtypeStruct((XC, 2, FW, BLK), BF),
+        compiler_params=ROOM,
         name="dense",
-    )(sums, w1, b1_wide, w2_half)
+    )(sums, w1, b1[None, :], w2_half)
     z = lax.all_to_all(z, ("x", "c"), 0, 0, tiled=True).reshape(ROWS, FW, BLK)
 
-    msg2 = quad_exchange(slot_terms(q, cols, counts, rows, z, tiles, False))
+    msg2 = quad_exchange(slot_terms((cols, counts), z, tiles))
     far = pl.pallas_call(
         functools.partial(second_sum_kernel, 1),
         in_specs=[VMEM] * 2,
         out_specs=VMEM,
         out_shape=jax.ShapeDtypeStruct((ROWS * FW, BLK), BF),
+        compiler_params=ROOM,
         name="far_sum",
     )(msg2, msg1)
     far = lax.ppermute(far, "q", [(0, 1), (1, 0)])
@@ -153,6 +187,7 @@
         in_specs=[VMEM] * 3,
         out_specs=VMEM,
         out_shape=jax.ShapeDtypeStruct((ROWS * FW, BLK), F32),
+        compiler_params=ROOM,
         name="near_sum",
     )(msg2, msg1, b2_wide)
     return (near + far.astype(F32)).reshape(ROWS, FW, BLK)

time: 130 us -> 116 us (0.89)
  the two profiles are of different devices: /device:TPU:2 before, /device:TPU:1 now
where the time goes in v2:
time: 116 us; the launch traced here: 115 us
  waiting for transfers between devices  46.8 us (40%)
  starting transfers between devices  28.7 us (25%)
  blocking collectives  28.7 us (25%)
  Pallas kernels  9.91 us (9%)
    all_to_all x1, blocking collectives, quad_exchange(): return lax.all_to_all(msg, ('y', 'b'), 0, 0, tiled=True)  21.3 us
    all_to_all x1, waiting for transfers between devices, per_device(): sums = lax.all_to_all(sums, ('q', 'h', 'x', 'c'), 0, 0, tiled=True)  20.5 us
    all_to_all x1, waiting for transfers between devices, quad_exchange(): return lax.all_to_all(msg, ('y', 'b'), 0, 0, tiled=True)  17.1 us
    all_to_all x1, starting transfers between devices, per_device(): sums = lax.all_to_all(sums, ('q', 'h', 'x', 'c'), 0, 0, tiled=True)  16.9 us
    all_to_all x1, starting transfers between devices, quad_exchange(): return lax.all_to_all(msg, ('y', 'b'), 0, 0, tiled=True)  9.19 us
    ppermute x1, waiting for transfers between devices, per_device(): far = lax.ppermute(far, 'q', [(0, 1), (1, 0)])  9.17 us
    pallas_call x2, Pallas kernels, slot_terms(): pl.pallas_call(functools.partial(terms_kernel, with_meta), in_specs=[hbm]...  7.82 us
    all_to_all x1, blocking collectives, per_device(): z = lax.all_to_all(z, ('x', 'c'), 0, 0, tiled=True).reshape(ROWS, FW, BLK)  7.4 us
  transfers between devices with their start and end apart: 3, of which 3 were waited for; matrix products, arithmetic and copies ran while one was open for 0% of the time, Pallas kernels for 0%

profile of v2, /device:TPU:1, one launch (start us, length us, event | category | flops | bytes accessed | tf_op | source)
XLA Modules:
  0.0 115.2 jit_solution(8854246264189240432)
XLA Ops:
  0.0 0.0 copy-start
  0.0 0.0 copy-start.1
  0.0 0.0 copy-start.2
  0.0 4.3 %slot_terms.2 = bf16[4,4,2,72,128]{4,3,2,1,0:T(8,128)(2,1)} custom-call(s32[1,4,32]{2,1,0:T(4,128)} %bitcast.12, s32[1,32]{1,0:T(1,128)} %refs_1_.3, s32[1,4,32]{2,1,0:T(4,128)} %bitcast.14, bf16[16,16,128]{2,1,0:T(8,128)(2,1)} %refs_3_.2, bf16[1,32,4,128,128]{4,3,2,1,0:T(8,128)(2,1)} %refs_3_.3), custom_call_target="tpu_custom_call" | custom-call | tf_op jit(solution)/shard_map/slot_terms/pallas_call | solution.py:68
  4.4 9.2 %all-to-all-start = ((bf16[16,144,128]{2,1,0:T(8,128)(2,1)}), bf16[16,144,128]{2,1,0:T(8,128)(2,1)S(1)}, u32[]{:S(2)}, u32[]{:S(2)}) async-start(bf16[16,144,128]{2,1,0:T(8,128)(2,1)} %bitcast.3), calls=%async_computation | async-start | bytes 1179648 | tf_op jit(solution)/shard_map/all_to_all | solution.py:152
  13.6 17.1 %all-to-all-done.msg_ref.meta_ref = bf16[16,144,128]{2,1,0:T(8,128)(2,1)S(1)} async-done(((bf16[16,144,128]{2,1,0:T(8,128)(2,1)}), bf16[16,144,128]{2,1,0:T(8,128)(2,1)S(1)}, u32[]{:S(2)}, u32[]{:S(2)}) %all-to-all-start) | async-done | bytes 589856 | tf_op jit(solution)/shard_map/all_to_all | solution.py:152
  30.7 1.1 first_sum.1
  31.8 0.0 copy-start.3
  31.8 16.9 %all-to-all-start.1 = ((bf16[32,32,128]{2,1,0:T(8,128)(2,1)}), bf16[32,32,128]{2,1,0:T(8,128)(2,1)S(1)}, u32[]{:S(2)}, u32[]{:S(2)}) async-start(bf16[32,32,128]{2,1,0:T(8,128)(2,1)} %bitcast.4), calls=%async_computation.1 | async-start | bytes 524288 | tf_op jit(solution)/shard_map/all_to_all | solution.py:164
  48.7 0.0 copy-done
  48.7 20.5 %all-to-all-done.1.agg_ref = bf16[32,32,128]{2,1,0:T(8,128)(2,1)S(1)} async-done(((bf16[32,32,128]{2,1,0:T(8,128)(2,1)}), bf16[32,32,128]{2,1,0:T(8,128)(2,1)S(1)}, u32[]{:S(2)}, u32[]{:S(2)}) %all-to-all-start.1) | async-done | bytes 262176 | tf_op jit(solution)/shard_map/all_to_all | solution.py:164
  69.2 0.0 copy-done.1
  69.2 0.0 copy-done.2
  69.2 0.4 dense.1
  69.6 7.4 %all_to_all.20 = bf16[8,2,16,128]{3,2,1,0:T(8,128)(2,1)S(1)} all-to-all(bf16[8,2,16,128]{3,2,1,0:T(8,128)(2,1)S(1)} %dense.1), channel_id=1, replica_groups=mesh['q'=2,'b'=4,'y'=4,'h'=2,'x'=4,'c'=2] {'x','c'}, dimensions={0} | all-to-all | bytes 131072 | tf_op jit(solution)/shard_map/all_to_all | solution.py:173
  77.0 3.5 %slot_terms.3 = bf16[4,4,2,64,128]{4,3,2,1,0:T(8,128)(2,1)S(1)} custom-call(s32[1,4,32]{2,1,0:T(4,128)} %bitcast.13, s32[1,32]{1,0:T(1,128)} %refs_1_.3, bf16[16,16,128]{2,1,0:T(8,128)(2,1)S(1)} %bitcast.10, bf16[1,32,4,128,128]{4,3,2,1,0:T(8,128)(2,1)} %refs_3_.3), custom_call_target="tpu_custom_call" | custom-call | tf_op jit(solution)/shard_map/slot_terms/pallas_call | solution.py:68
  80.5 21.3 %all_to_all.21.msg_ref = bf16[16,128,128]{2,1,0:T(8,128)(2,1)S(1)} all-to-all(bf16[16,128,128]{2,1,0:T(8,128)(2,1)S(1)} %bitcast.9), channel_id=1, replica_groups=mesh['q'=2,'b'=4,'y'=4,'h'=2,'x'=4,'c'=2] {'y','b'}, dimensions={0} | all-to-all | bytes 1048576 | tf_op jit(solution)/shard_map/all_to_all | solution.py:152
  101.8 0.3 far_sum.1
  102.1 2.6 %collective-permute-start = (bf16[256,128]{1,0:T(8,128)(2,1)S(1)}, bf16[256,128]{1,0:T(8,128)(2,1)S(1)}, u32[]{:S(2)}, u32[]{:S(2)}) collective-permute-start(bf16[256,128]{1,0:T(8,128)(2,1)S(1)} %far_sum.1), channel_id=1, source_target_pairs={{0,256},{256,0},{1,257},{257,1},{2,258},{258,2},{3,259},{259,3},{4... | collective-permute-start | bytes 196616 | tf_op jit(solution)/shard_map/ppermute | solution.py:184
  104.7 0.0 copy-done.3
  104.7 0.1 dynamic_slice.7
  104.8 0.1 broadcast_in_dim.15
  104.9 0.1 broadcast_in_dim.16.refs_0_
  105.0 0.3 near_sum.1
  105.3 9.2 %collective-permute-done = bf16[256,128]{1,0:T(8,128)(2,1)S(1)} collective-permute-done((bf16[256,128]{1,0:T(8,128)(2,1)S(1)}, bf16[256,128]{1,0:T(8,128)(2,1)S(1)}, u32[]{:S(2)}, u32[]{:S(2)}) %collective-permute-start) | collective-permute-done | bytes 65568 | tf_op jit(solution)/shard_map/ppermute | solution.py:184
  114.5 0.7 convert_add_fusion
  (2 shorter events, 0.0 us)
Async XLA Ops:
  0.0 48.7 %copy-start = (bf16[256,256]{1,0:T(8,128)(2,1)S(1)}, bf16[256,256]{1,0:T(8,128)(2,1)}, u32[]{:S(2)}) copy-start(bf16[256,256]{1,0:T(8,128)(2,1)} %param.16) | copy-start | bytes 393220
  0.0 69.2 %copy-start.1 = (bf16[256,256]{1,0:T(8,128)(2,1)S(1)}, bf16[256,256]{1,0:T(8,128)(2,1)}, u32[]{:S(2)}) copy-start(bf16[256,256]{1,0:T(8,128)(2,1)} %w1_ref.1) | copy-start | bytes 393220
  0.0 69.2 %copy-start.2 = (f32[256]{0:T(256)S(1)}, f32[256]{0:T(256)}, u32[]{:S(2)}) copy-start(f32[256]{0:T(256)} %param.15) | copy-start | bytes 3076
  4.4 26.3 %all-to-all-start = ((bf16[16,144,128]{2,1,0:T(8,128)(2,1)}), bf16[16,144,128]{2,1,0:T(8,128)(2,1)S(1)}, u32[]{:S(2)}, u32[]{:S(2)}) async-start(bf16[16,144,128]{2,1,0:T(8,128)(2,1)} %bitcast.3), calls=%async_computation | async-start | bytes 1179648 | tf_op jit(solution)/shard_map/all_to_all | solution.py:152
  31.8 72.9 %copy-start.3 = (f32[256]{0:T(256)S(1)}, f32[256]{0:T(256)}, u32[]{:S(2)}) copy-start(f32[256]{0:T(256)} %param.17) | copy-start | bytes 3076
  31.8 37.4 %all-to-all-start.1 = ((bf16[32,32,128]{2,1,0:T(8,128)(2,1)}), bf16[32,32,128]{2,1,0:T(8,128)(2,1)S(1)}, u32[]{:S(2)}, u32[]{:S(2)}) async-start(bf16[32,32,128]{2,1,0:T(8,128)(2,1)} %bitcast.4), calls=%async_computation.1 | async-start | bytes 524288 | tf_op jit(solution)/shard_map/all_to_all | solution.py:164
  102.1 12.4 %collective-permute-start = (bf16[256,128]{1,0:T(8,128)(2,1)S(1)}, bf16[256,128]{1,0:T(8,128)(2,1)S(1)}, u32[]{:S(2)}, u32[]{:S(2)}) collective-permute-start(bf16[256,128]{1,0:T(8,128)(2,1)S(1)} %far_sum.1), channel_id=1, source_target_pairs={{0,256},{256,0},{1,257},{257,1},{2,258},{258,2},{3,259},{259,3},{4... | collective-permute-start | bytes 196616 | tf_op jit(solution)/shard_map/ppermute | solution.py:184

commit v3 on v0

v3 whole, which is shorter than its diff:
```python
import functools

import jax
import jax.numpy as jnp
from jax import lax
from jax.experimental import pallas as pl
from jax.experimental.pallas import tpu as pltpu
from jax.sharding import Mesh
from jax.sharding import PartitionSpec as P

QUADS, ZQ, YS, HS, XS, CS = 2, 4, 4, 2, 4, 2
XC = XS * CS
STEPS = QUADS * ZQ
CAP, BLK, FW, ROWS = 4, 128, 16, 16
MSG = CAP * FW
BODY = QUADS * MSG
META = 8
LINES = ROWS * FW
BF, F32 = jnp.bfloat16, jnp.float32
VMEM = pl.BlockSpec(memory_space=pltpu.VMEM)
HBM = pl.BlockSpec(memory_space=pltpu.HBM)
NT = (((1,), (1,)), ((), ()))
TN = (((0,), (0,)), ((), ()))
ROOM = pltpu.CompilerParams(vmem_limit_bytes=8 << 20)


def in_hbm(array):
    return pltpu.with_memory_space_constraint(array, pltpu.HBM)


def target(step, y):
    q = lax.axis_index("q").astype(jnp.int32)
    return ((step // ZQ ^ q) * ZQ + step % ZQ) * YS + y


def write_terms(step, cols_ref, counts_ref, values_ref, tiles_ref, out_ref):
    for y in range(YS):
        p = target(step, y)
        count = counts_ref[0, p]
        for j in range(0, CAP, 2):
            pair = jnp.concatenate([values_ref[cols_ref[0, j + i, p]] for i in range(2)], axis=0)
            tiles = tiles_ref[step, y, j : j + 2].reshape(2 * BLK, BLK)
            term = lax.dot_general(pair, tiles, NT, preferred_element_type=F32)
            for i in range(2):
                mine = term[i * FW : (i + 1) * FW, i * BLK : (i + 1) * BLK]
                mine = jnp.where(j + i < count, mine, 0.0).astype(BF)
                at = (step // ZQ) * MSG + (j + i) * FW
                out_ref[y, step % ZQ, at : at + FW, :] = mine


def first_terms_kernel(
    cols_in, counts_in, rows_in, values_in, tiles_in, out_ref, tiles_ref, cols, counts, rows, values, sems
):
    small = list(zip((cols_in, counts_in, rows_in, values_in), (cols, counts, rows, values)))
    copies = [pltpu.make_async_copy(src, dst, sems.at[i]) for i, (src, dst) in enumerate(small)]
    for step in range(STEPS):
        chunk = tiles_in.at[0, pl.ds(target(step, 0), YS)]
        copies.append(pltpu.make_async_copy(chunk, tiles_ref.at[step], sems.at[len(copies)]))
    for copy in copies:
        copy.start()
    for copy in copies[: len(small)]:
        copy.wait()
    lane = lax.broadcasted_iota(jnp.int32, (META, BLK), 1)
    for b in range(ZQ):
        for y in range(YS):
            place = lane % FW
            for r in range(QUADS):
                for j in range(CAP):
                    row = rows[0, j, target(r * ZQ + b, y)]
                    place = jnp.where(lane // FW == r * CAP + j, place + row * FW, place)
            out_ref[y, b, BODY:, :] = place.astype(F32).astype(BF)
    for step in range(STEPS):
        copies[len(small) + step].wait()
        write_terms(step, cols, counts, values, tiles_ref, out_ref)


def second_terms_kernel(cols_in, counts_in, values_ref, tiles_ref, out_ref, cols, counts, sems):
    copies = [pltpu.make_async_copy(cols_in, cols, sems.at[0]), pltpu.make_async_copy(counts_in, counts, sems.at[1])]
    for copy in copies:
        copy.start()
    for copy in copies:
        copy.wait()
    for step in range(STEPS):
        write_terms(step, cols, counts, values_ref, tiles_ref, out_ref)


def placed_sum(r, msg_ref, meta_ref):
    total = jnp.zeros((LINES, BLK), F32)
    low = lax.broadcasted_iota(jnp.int32, (META, BLK), 1) < MSG
    spot = lax.broadcasted_iota(jnp.int32, (LINES, BLK), 0).astype(F32)
    for s in range(0, YS * ZQ, 4):
        halves = []
        for t in (s, s + 2):
            here, there = (meta_ref[t + i, BODY:, :].astype(F32) for i in range(2))
            if r == 0:
                there = pltpu.roll(there, MSG, 1)
            else:
                here = pltpu.roll(here, MSG, 1)
            place = jnp.concatenate([jnp.where(low, here, there)] * (LINES // META), axis=0)
            halves.append(jnp.where(spot == place, 1.0, 0.0).astype(BF))
        put = jnp.concatenate(halves, axis=1)
        lines = jnp.concatenate([msg_ref[s + i, r * MSG : (r + 1) * MSG, :] for i in range(4)], axis=0)
        total += jnp.dot(put, lines, preferred_element_type=F32)
    return total


def first_sum_kernel(msg_ref, out_ref):
    for r in range(QUADS):
        total = placed_sum(r, msg_ref, msg_ref).astype(BF)
        for h in range(HS):
            out_ref[r ^ lax.axis_index("q").astype(jnp.int32), h] = total


def far_sum_kernel(msg_ref, meta_ref, out_ref):
    out_ref[...] = placed_sum(1, msg_ref, meta_ref).astype(BF)


def column(bias_ref):
    return jnp.transpose(jnp.broadcast_to(bias_ref[...], (BLK, bias_ref.shape[1])))


def near_sum_kernel(msg_ref, meta_ref, bias_ref, out_ref, wide):
    wide[...] = column(bias_ref)
    h, x, c = (lax.axis_index(name).astype(jnp.int32) for name in ("h", "x", "c"))
    own = pl.multiple_of(((h * XS + x) * CS + c) * FW, FW)
    bias = jnp.concatenate([wide[pl.ds(own, FW), :]] * ROWS, axis=0)
    out_ref[...] = placed_sum(0, msg_ref, meta_ref) + bias


def dense_kernel(agg_ref, w1_ref, b1_ref, w2_ref, out_ref):
    half = agg_ref.shape[0] // 2
    agg = agg_ref[:half].astype(F32) + agg_ref[half:].astype(F32)
    agg = jnp.concatenate([agg[:, i * FW : (i + 1) * FW, :].reshape(half * FW, BLK) for i in range(2)], axis=1)
    hidden = lax.dot_general(w1_ref[...], agg.astype(BF), TN, preferred_element_type=F32)
    bias = column(b1_ref)
    hidden = jnp.maximum(hidden + jnp.concatenate([bias, bias], axis=1), 0.0).astype(BF)
    own = pl.multiple_of(lax.axis_index("h").astype(jnp.int32) * (XC * FW), XC * FW)
    out = lax.dot_general(w2_ref[:, pl.ds(own, XC * FW)], hidden, TN, preferred_element_type=F32).astype(BF)
    for i in range(2):
        out_ref[:, i] = out[:, i * BLK : (i + 1) * BLK].reshape(XC, FW, BLK)


def call(kernel, name, out_shape, *args, in_specs=None, scratch_shapes=()):
    return pl.pallas_call(
        kernel,
        in_specs=in_specs or [VMEM] * len(args),
        out_specs=jax.tree.map(lambda _: VMEM, out_shape),
        out_shape=out_shape,
        scratch_shapes=scratch_shapes,
        compiler_params=ROOM,
        name=name,
    )(*args)


def per_device(features, tiles, rows, cols, counts, w1, b1, w2, b2):
    cols, rows = (jnp.swapaxes(table, 1, 2) for table in (cols, rows))
    cols, rows, counts, features, tiles = (in_hbm(array) for array in (cols, rows, counts, features, tiles))
    b1, b2 = b1[None, :], b2[None, :]
    smem = [pltpu.SMEM(table.shape, table.dtype) for table in (cols, counts, rows)]
    copy_sems = pltpu.SemaphoreType.DMA

    def message(lines):
        return jax.ShapeDtypeStruct((YS, ZQ, lines, BLK), BF)

    def quad_exchange(msg):
        msg = msg.reshape(YS * ZQ, msg.shape[2], BLK)
        return lax.all_to_all(msg, ("y", "b"), 0, 0, tiled=True)

    msg1, held = call(
        first_terms_kernel,
        "first_terms",
        (message(BODY + META), pltpu.VMEM((STEPS, YS, CAP, BLK, BLK), BF)),
        cols,
        counts,
        rows,
        features,
        tiles,
        in_specs=[HBM] * 5,
        scratch_shapes=[*smem, pltpu.VMEM(features.shape, BF), copy_sems((4 + STEPS,))],
    )
    msg1 = quad_exchange(msg1)
    sums = call(first_sum_kernel, "first_sum", jax.ShapeDtypeStruct((QUADS, HS, LINES, BLK), BF), msg1)
    sums = sums.reshape(QUADS * HS * XC, 2 * FW, BLK)
    sums = lax.all_to_all(sums, ("q", "h", "x", "c"), 0, 0, tiled=True)
    z = call(dense_kernel, "dense", jax.ShapeDtypeStruct((XC, 2, FW, BLK), BF), sums, w1, b1, w2)
    z = lax.all_to_all(z, ("x", "c"), 0, 0, tiled=True).reshape(ROWS, FW, BLK)

    msg2 = call(
        second_terms_kernel,
        "second_terms",
        message(BODY),
        cols,
        counts,
        z,
        held,
        in_specs=[HBM, HBM, VMEM, VMEM],
        scratch_shapes=[*smem[:2], copy_sems((2,))],
    )
    msg2 = quad_exchange(msg2)
    far = call(far_sum_kernel, "far_sum", jax.ShapeDtypeStruct((LINES, BLK), BF), msg2, msg1)
    far = lax.ppermute(far, "q", [(0, 1), (1, 0)])
    near = call(
        near_sum_kernel,
        "near_sum",
        jax.ShapeDtypeStruct((LINES, BLK), F32),
        msg2,
        msg1,
        b2,
        scratch_shapes=[pltpu.VMEM((b2.shape[1], BLK), F32)],
    )
    return (near + far.astype(F32)).reshape(ROWS, FW, BLK)


def solution(mesh):
    fine = Mesh(mesh.devices.reshape(QUADS, ZQ, YS, HS, XS, CS), ("q", "b", "y", "h", "x", "c"))
    dom, feat = ("q", "b", "y"), ("h", "x", "c")
    placed = (
        P(dom, feat, None),
        P(dom, None, None, None, None),
        P(dom, None, None),
        P(dom, None, None),
        P(dom, None),
        P(),
        P(),
        P(),
        P(),
    )
    return jax.shard_map(
        per_device, mesh=fine, in_specs=placed, out_specs=P(dom, feat, None), check_vma=False
    )
```

time: 602 us -> 112 us (0.19)
  waiting for transfers between devices: 436 us -> 9.37 us
  blocking collectives: 129 us -> 91.8 us
  matrix products: 13.9 us -> 0 us
  between operations: 13.5 us -> 0.08 us
  Pallas kernels: 0 us -> 7.35 us
    reduce_scatter x2 -> x0, waiting for transfers between devices: 436 us -> none  [aggregate(): lax.psum_scatter(placed.reshape(lax.axis_size('dom') * blocks_here, sourc...]
    all_to_all x4, blocking collectives: 129 us -> 91.8 us  [the longest x2 46.9 us: quad_exchange(): return lax.all_to_all(msg, ('y', 'b'), 0, 0, tiled=True)]
    dot_general x8 -> x0, matrix products: 13.9 us -> none  [the longest x2 8.94 us: slot_terms(): jnp.einsum('pjfk,pjik->pjfi', selected, tile_set, preferred_element_type=...]
    ppermute x0 -> x1, waiting for transfers between devices: none -> 9.37 us  [per_device(): far = lax.ppermute(far, 'q', [(0, 1), (1, 0)])]
    pallas_call x0 -> x6, Pallas kernels: none -> 7.35 us  [call(): pl.pallas_call(kernel, in_specs=in_specs or [VMEM] * len(args), out_specs...]
  transfers between devices with their start and end apart: 2 -> 1, of which waited for: 2 -> 1; matrix products, arithmetic and copies ran while one was open for 0% -> 0% of each run, Pallas kernels for 0% -> 0%
where the time goes in v3:
time: 112 us
  blocking collectives  91.8 us (82%)
  waiting for transfers between devices  9.37 us (8%)
  Pallas kernels  7.35 us (7%)
  starting transfers between devices  2.64 us (2%)
    all_to_all x2, blocking collectives, quad_exchange(): return lax.all_to_all(msg, ('y', 'b'), 0, 0, tiled=True)  46.9 us
    all_to_all x1, blocking collectives, per_device(): sums = lax.all_to_all(sums, ('q', 'h', 'x', 'c'), 0, 0, tiled=True)  37.9 us
    ppermute x1, waiting for transfers between devices, per_device(): far = lax.ppermute(far, 'q', [(0, 1), (1, 0)])  9.37 us
    pallas_call x6, Pallas kernels, call(): pl.pallas_call(kernel, in_specs=in_specs or [VMEM] * len(args), out_specs...  7.35 us
    all_to_all x1, blocking collectives, per_device(): z = lax.all_to_all(z, ('x', 'c'), 0, 0, tiled=True).reshape(ROWS, FW, BLK)  7.08 us
    ppermute x1, starting transfers between devices, per_device(): far = lax.ppermute(far, 'q', [(0, 1), (1, 0)])  2.64 us
  transfers between devices with their start and end apart: 1, of which 1 were waited for; matrix products, arithmetic and copies ran while one was open for 0% of the time, Pallas kernels for 0%

profile of v3, /device:TPU:1, one launch (start us, length us, event | category | flops | bytes accessed | tf_op | source)
XLA Modules:
  0.0 111.9 jit_solution(11263831505970532548)
XLA Ops:
  0.0 0.0 copy-start.1
  0.0 0.0 copy-start.2
  0.0 0.0 copy-start
  0.0 3.5 %first_terms.1 = (bf16[4,4,136,128]{3,2,1,0:T(8,128)(2,1)S(1)}, bf16[8,4,4,128,128]{4,3,2,1,0:T(8,128)(2,1)S(1)}) custom-call(s32[1,4,32]{2,1,0:T(4,128)} %bitcast.15, s32[1,32]{1,0:T(1,128)} %counts_in.3, s32[1,4,32]{2,1,0:T(4,128)} %bitcast.17, bf16[16,16,128]{2,1,0:T(8,128)(2,1)} %values_in.1, bf16[1,32,4,128,128]{4,3,2,1,0:T(8,128)(2,1)} %tiles_in.1), custom_call_target="tpu_custom_call" | custom-call | tf_op jit(solution)/shard_map/first_terms/pallas_call | solution.py:144
  3.5 25.4 %all_to_all.20.msg_ref.meta_ref = bf16[16,136,128]{2,1,0:T(8,128)(2,1)S(1)} all-to-all(bf16[16,136,128]{2,1,0:T(8,128)(2,1)S(1)} %bitcast.11), channel_id=1, replica_groups=mesh['q'=2,'b'=4,'y'=4,'h'=2,'x'=4,'c'=2] {'y','b'}, dimensions={0} | all-to-all | bytes 1114112 | tf_op jit(solution)/shard_map/all_to_all | solution.py:167
  28.9 0.5 first_sum.1
  29.4 0.0 copy-start.3
  29.4 37.9 %all_to_all.21.agg_ref = bf16[32,32,128]{2,1,0:T(8,128)(2,1)S(1)} all-to-all(bf16[32,32,128]{2,1,0:T(8,128)(2,1)S(1)} %bitcast.10), channel_id=1, replica_groups=mesh['q'=2,'b'=4,'y'=4,'h'=2,'x'=4,'c'=2] {'q','h','x','c'}, dimensions={0} | all-to-all | bytes 524288 | tf_op jit(solution)/shard_map/all_to_all | solution.py:184
  67.3 0.0 copy-done.1
  67.3 0.0 copy-done.2
  67.3 0.0 copy-done
  67.3 0.4 dense.1
  67.7 7.1 %all_to_all.22 = bf16[8,2,16,128]{3,2,1,0:T(8,128)(2,1)S(1)} all-to-all(bf16[8,2,16,128]{3,2,1,0:T(8,128)(2,1)S(1)} %dense.1), channel_id=1, replica_groups=mesh['q'=2,'b'=4,'y'=4,'h'=2,'x'=4,'c'=2] {'x','c'}, dimensions={0} | all-to-all | bytes 131072 | tf_op jit(solution)/shard_map/all_to_all | solution.py:186
  74.8 2.3 %second_terms.1 = bf16[4,4,128,128]{3,2,1,0:T(8,128)(2,1)S(1)} custom-call(s32[1,4,32]{2,1,0:T(4,128)} %bitcast.16, s32[1,32]{1,0:T(1,128)} %counts_in.3, bf16[16,16,128]{2,1,0:T(8,128)(2,1)S(1)} %bitcast.12, bf16[8,4,4,128,128]{4,3,2,1,0:T(8,128)(2,1)S(1)} %get-tuple-element.8.tiles_ref), custom_call_target="tpu_custom_call" | custom-call | tf_op jit(solution)/shard_map/second_terms/pallas_call | solution.py:144
  77.0 21.5 %all_to_all.23.msg_ref = bf16[16,128,128]{2,1,0:T(8,128)(2,1)S(1)} all-to-all(bf16[16,128,128]{2,1,0:T(8,128)(2,1)S(1)} %bitcast.9), channel_id=1, replica_groups=mesh['q'=2,'b'=4,'y'=4,'h'=2,'x'=4,'c'=2] {'y','b'}, dimensions={0} | all-to-all | bytes 1048576 | tf_op jit(solution)/shard_map/all_to_all | solution.py:167
  98.5 0.3 far_sum.1
  98.9 2.6 %collective-permute-start = (bf16[256,128]{1,0:T(8,128)(2,1)S(1)}, bf16[256,128]{1,0:T(8,128)(2,1)S(1)}, u32[]{:S(2)}, u32[]{:S(2)}) collective-permute-start(bf16[256,128]{1,0:T(8,128)(2,1)S(1)} %far_sum.1), channel_id=1, source_target_pairs={{0,256},{256,0},{1,257},{257,1},{2,258},{258,2},{3,259},{259,3},{4... | collective-permute-start | bytes 196616 | tf_op jit(solution)/shard_map/ppermute | solution.py:201
  101.5 0.0 copy-done.3
  101.5 0.4 near_sum.1
  101.9 9.4 %collective-permute-done = bf16[256,128]{1,0:T(8,128)(2,1)S(1)} collective-permute-done((bf16[256,128]{1,0:T(8,128)(2,1)S(1)}, bf16[256,128]{1,0:T(8,128)(2,1)S(1)}, u32[]{:S(2)}, u32[]{:S(2)}) %collective-permute-start) | collective-permute-done | bytes 65568 | tf_op jit(solution)/shard_map/ppermute | solution.py:201
  111.3 0.7 convert_add_fusion
Async XLA Ops:
  0.0 67.3 %copy-start.1 = (bf16[256,256]{1,0:T(8,128)(2,1)S(1)}, bf16[256,256]{1,0:T(8,128)(2,1)}, u32[]{:S(2)}) copy-start(bf16[256,256]{1,0:T(8,128)(2,1)} %w2_ref.1) | copy-start | bytes 393220
  0.0 67.3 %copy-start.2 = (f32[256]{0:T(256)S(1)}, f32[256]{0:T(256)}, u32[]{:S(2)}) copy-start(f32[256]{0:T(256)} %param.15) | copy-start | bytes 3076
  0.0 67.3 %copy-start = (bf16[256,256]{1,0:T(8,128)(2,1)S(1)}, bf16[256,256]{1,0:T(8,128)(2,1)}, u32[]{:S(2)}) copy-start(bf16[256,256]{1,0:T(8,128)(2,1)} %w1_ref.1) | copy-start | bytes 393220
  29.4 72.1 %copy-start.3 = (f32[256]{0:T(256)S(1)}, f32[256]{0:T(256)}, u32[]{:S(2)}) copy-start(f32[256]{0:T(256)} %param.17) | copy-start | bytes 3076
  98.9 12.4 %collective-permute-start = (bf16[256,128]{1,0:T(8,128)(2,1)S(1)}, bf16[256,128]{1,0:T(8,128)(2,1)S(1)}, u32[]{:S(2)}, u32[]{:S(2)}) collective-permute-start(bf16[256,128]{1,0:T(8,128)(2,1)S(1)} %far_sum.1), channel_id=1, source_target_pairs={{0,256},{256,0},{1,257},{257,1},{2,258},{258,2},{3,259},{259,3},{4... | collective-permute-start | bytes 196616 | tf_op jit(solution)/shard_map/ppermute | solution.py:201

commit v4 on v3

--- a/solution.py
+++ b/solution.py
@@ -11,6 +11,7 @@
 QUADS, ZQ, YS, HS, XS, CS = 2, 4, 4, 2, 4, 2
 XC = XS * CS
 STEPS = QUADS * ZQ
+WAVE = 2
 CAP, BLK, FW, ROWS = 4, 128, 16, 16
 MSG = CAP * FW
 BODY = QUADS * MSG
@@ -45,7 +46,7 @@
                 mine = term[i * FW : (i + 1) * FW, i * BLK : (i + 1) * BLK]
                 mine = jnp.where(j + i < count, mine, 0.0).astype(BF)
                 at = (step // ZQ) * MSG + (j + i) * FW
-                out_ref[y, step % ZQ, at : at + FW, :] = mine
+                out_ref[step % ZQ, y, at : at + FW, :] = mine
 
 
 def first_terms_kernel(
@@ -53,9 +54,9 @@
 ):
     small = list(zip((cols_in, counts_in, rows_in, values_in), (cols, counts, rows, values)))
     copies = [pltpu.make_async_copy(src, dst, sems.at[i]) for i, (src, dst) in enumerate(small)]
-    for step in range(STEPS):
-        chunk = tiles_in.at[0, pl.ds(target(step, 0), YS)]
-        copies.append(pltpu.make_async_copy(chunk, tiles_ref.at[step], sems.at[len(copies)]))
+    for step in range(0, STEPS, WAVE):
+        chunk = tiles_in.at[0, pl.ds(target(step, 0) // YS, WAVE)]
+        copies.append(pltpu.make_async_copy(chunk, tiles_ref.at[pl.ds(step, WAVE)], sems.at[len(copies)]))
     for copy in copies:
         copy.start()
     for copy in copies[: len(small)]:
@@ -68,9 +69,10 @@
                 for j in range(CAP):
                     row = rows[0, j, target(r * ZQ + b, y)]
                     place = jnp.where(lane // FW == r * CAP + j, place + row * FW, place)
-            out_ref[y, b, BODY:, :] = place.astype(F32).astype(BF)
+            out_ref[b, y, BODY:, :] = place.astype(F32).astype(BF)
     for step in range(STEPS):
-        copies[len(small) + step].wait()
+        if step % WAVE == 0:
+            copies[len(small) + step // WAVE].wait()
         write_terms(step, cols, counts, values, tiles_ref, out_ref)
 
 
@@ -88,7 +90,7 @@
     total = jnp.zeros((LINES, BLK), F32)
     low = lax.broadcasted_iota(jnp.int32, (META, BLK), 1) < MSG
     spot = lax.broadcasted_iota(jnp.int32, (LINES, BLK), 0).astype(F32)
-    for s in range(0, YS * ZQ, 4):
+    for s in range(0, ZQ * YS, 4):
         halves = []
         for t in (s, s + 2):
             here, there = (meta_ref[t + i, BODY:, :].astype(F32) for i in range(2))
@@ -154,17 +156,17 @@
 
 def per_device(features, tiles, rows, cols, counts, w1, b1, w2, b2):
     cols, rows = (jnp.swapaxes(table, 1, 2) for table in (cols, rows))
-    cols, rows, counts, features, tiles = (in_hbm(array) for array in (cols, rows, counts, features, tiles))
+    cols, rows, counts, features = (in_hbm(array) for array in (cols, rows, counts, features))
     b1, b2 = b1[None, :], b2[None, :]
     smem = [pltpu.SMEM(table.shape, table.dtype) for table in (cols, counts, rows)]
     copy_sems = pltpu.SemaphoreType.DMA
 
     def message(lines):
-        return jax.ShapeDtypeStruct((YS, ZQ, lines, BLK), BF)
+        return jax.ShapeDtypeStruct((ZQ, YS, lines, BLK), BF)
 
     def quad_exchange(msg):
-        msg = msg.reshape(YS * ZQ, msg.shape[2], BLK)
-        return lax.all_to_all(msg, ("y", "b"), 0, 0, tiled=True)
+        msg = msg.reshape(ZQ * YS, msg.shape[2], BLK)
+        return lax.all_to_all(msg, ("b", "y"), 0, 0, tiled=True)
 
     msg1, held = call(
         first_terms_kernel,
@@ -174,9 +176,9 @@
         counts,
         rows,
         features,
-        tiles,
+        in_hbm(tiles.reshape(1, STEPS, YS, CAP, BLK, BLK)),
         in_specs=[HBM] * 5,
-        scratch_shapes=[*smem, pltpu.VMEM(features.shape, BF), copy_sems((4 + STEPS,))],
+        scratch_shapes=[*smem, pltpu.VMEM(features.shape, BF), copy_sems((4 + STEPS // WAVE,))],
     )
     msg1 = quad_exchange(msg1)
     sums = call(first_sum_kernel, "first_sum", jax.ShapeDtypeStruct((QUADS, HS, LINES, BLK), BF), msg1)

time: 112 us -> 111 us (level)
  the two profiles are of different devices: /device:TPU:1 before, /device:TPU:2 now
where the time goes in v4:
time: 111 us; the launch traced here: 110 us
  blocking collectives  90.3 us (81%)
  waiting for transfers between devices  9.2 us (8%)
  Pallas kernels  7.08 us (6%)
  starting transfers between devices  2.96 us (3%)
    all_to_all x2, blocking collectives, quad_exchange(): return lax.all_to_all(msg, ('b', 'y'), 0, 0, tiled=True)  47.4 us
    all_to_all x1, blocking collectives, per_device(): sums = lax.all_to_all(sums, ('q', 'h', 'x', 'c'), 0, 0, tiled=True)  34.7 us
    ppermute x1, waiting for transfers between devices, per_device(): far = lax.ppermute(far, 'q', [(0, 1), (1, 0)])  9.2 us
    all_to_all x1, blocking collectives, per_device(): z = lax.all_to_all(z, ('x', 'c'), 0, 0, tiled=True).reshape(ROWS, FW, BLK)  8.14 us
    pallas_call x6, Pallas kernels, call(): pl.pallas_call(kernel, in_specs=in_specs or [VMEM] * len(args), out_specs...  7.08 us
    ppermute x1, starting transfers between devices, per_device(): far = lax.ppermute(far, 'q', [(0, 1), (1, 0)])  2.96 us
  transfers between devices with their start and end apart: 1, of which 1 were waited for; matrix products, arithmetic and copies ran while one was open for 0% of the time, Pallas kernels for 0%

profile of v4, /device:TPU:2, one launch (start us, length us, event | category | flops | bytes accessed | tf_op | source)
XLA Modules:
  0.0 110.3 jit_solution(40843201294539353)
XLA Ops:
  0.0 0.0 copy-start.1
  0.0 0.0 copy-start.2
  0.0 0.0 copy-start
  0.0 3.2 %first_terms.1 = (bf16[4,4,136,128]{3,2,1,0:T(8,128)(2,1)S(1)}, bf16[8,4,4,128,128]{4,3,2,1,0:T(8,128)(2,1)S(1)}) custom-call(s32[1,4,32]{2,1,0:T(4,128)} %bitcast.17, s32[1,32]{1,0:T(1,128)} %counts_in.3, s32[1,4,32]{2,1,0:T(4,128)} %bitcast.19, bf16[16,16,128]{2,1,0:T(8,128)(2,1)} %values_in.1, bf16[1,8,4,4,128,128]{5,4,3,2,1,0:T(8,128)(2,1)} %bitcast.16), custom_call_target="tpu_custom_call" | custom-call | tf_op jit(solution)/shard_map/first_terms/pallas_call | solution.py:146
  3.3 25.8 %all_to_all.20.msg_ref.meta_ref = bf16[16,136,128]{2,1,0:T(8,128)(2,1)S(1)} all-to-all(bf16[16,136,128]{2,1,0:T(8,128)(2,1)S(1)} %bitcast.12), channel_id=1, replica_groups=mesh['q'=2,'b'=4,'y'=4,'h'=2,'x'=4,'c'=2] {'b','y'}, dimensions={0} | all-to-all | bytes 1114112 | tf_op jit(solution)/shard_map/all_to_all | solution.py:169
  29.0 0.5 first_sum.1
  29.5 0.0 copy-start.3
  29.5 34.7 %all_to_all.21.agg_ref = bf16[32,32,128]{2,1,0:T(8,128)(2,1)S(1)} all-to-all(bf16[32,32,128]{2,1,0:T(8,128)(2,1)S(1)} %bitcast.11), channel_id=1, replica_groups=mesh['q'=2,'b'=4,'y'=4,'h'=2,'x'=4,'c'=2] {'q','h','x','c'}, dimensions={0} | all-to-all | bytes 524288 | tf_op jit(solution)/shard_map/all_to_all | solution.py:186
  64.3 0.0 copy-done.1
  64.3 0.0 copy-done.2
  64.3 0.0 copy-done
  64.3 0.4 dense.1
  64.7 8.1 %all_to_all.22 = bf16[8,2,16,128]{3,2,1,0:T(8,128)(2,1)S(1)} all-to-all(bf16[8,2,16,128]{3,2,1,0:T(8,128)(2,1)S(1)} %dense.1), channel_id=1, replica_groups=mesh['q'=2,'b'=4,'y'=4,'h'=2,'x'=4,'c'=2] {'x','c'}, dimensions={0} | all-to-all | bytes 131072 | tf_op jit(solution)/shard_map/all_to_all | solution.py:188
  72.8 2.3 %second_terms.1 = bf16[4,4,128,128]{3,2,1,0:T(8,128)(2,1)S(1)} custom-call(s32[1,4,32]{2,1,0:T(4,128)} %bitcast.18, s32[1,32]{1,0:T(1,128)} %counts_in.3, bf16[16,16,128]{2,1,0:T(8,128)(2,1)S(1)} %bitcast.13, bf16[8,4,4,128,128]{4,3,2,1,0:T(8,128)(2,1)S(1)} %get-tuple-element.8.tiles_ref), custom_call_target="tpu_custom_call" | custom-call | tf_op jit(solution)/shard_map/second_terms/pallas_call | solution.py:146
  75.1 21.6 %all_to_all.23.msg_ref = bf16[16,128,128]{2,1,0:T(8,128)(2,1)S(1)} all-to-all(bf16[16,128,128]{2,1,0:T(8,128)(2,1)S(1)} %bitcast.10), channel_id=1, replica_groups=mesh['q'=2,'b'=4,'y'=4,'h'=2,'x'=4,'c'=2] {'b','y'}, dimensions={0} | all-to-all | bytes 1048576 | tf_op jit(solution)/shard_map/all_to_all | solution.py:169
  96.7 0.4 far_sum.1
  97.1 3.0 %collective-permute-start = (bf16[256,128]{1,0:T(8,128)(2,1)S(1)}, bf16[256,128]{1,0:T(8,128)(2,1)S(1)}, u32[]{:S(2)}, u32[]{:S(2)}) collective-permute-start(bf16[256,128]{1,0:T(8,128)(2,1)S(1)} %far_sum.1), channel_id=1, source_target_pairs={{0,256},{256,0},{1,257},{257,1},{2,258},{258,2},{3,259},{259,3},{4... | collective-permute-start | bytes 196616 | tf_op jit(solution)/shard_map/ppermute | solution.py:203
  100.1 0.0 copy-done.3
  100.1 0.4 near_sum.1
  100.4 9.2 %collective-permute-done = bf16[256,128]{1,0:T(8,128)(2,1)S(1)} collective-permute-done((bf16[256,128]{1,0:T(8,128)(2,1)S(1)}, bf16[256,128]{1,0:T(8,128)(2,1)S(1)}, u32[]{:S(2)}, u32[]{:S(2)}) %collective-permute-start) | collective-permute-done | bytes 65568 | tf_op jit(solution)/shard_map/ppermute | solution.py:203
  109.7 0.7 convert_add_fusion
Async XLA Ops:
  0.0 64.3 %copy-start.1 = (bf16[256,256]{1,0:T(8,128)(2,1)S(1)}, bf16[256,256]{1,0:T(8,128)(2,1)}, u32[]{:S(2)}) copy-start(bf16[256,256]{1,0:T(8,128)(2,1)} %w2_ref.1) | copy-start | bytes 393220
  0.0 64.3 %copy-start.2 = (f32[256]{0:T(256)S(1)}, f32[256]{0:T(256)}, u32[]{:S(2)}) copy-start(f32[256]{0:T(256)} %param.15) | copy-start | bytes 3076
  0.0 64.3 %copy-start = (bf16[256,256]{1,0:T(8,128)(2,1)S(1)}, bf16[256,256]{1,0:T(8,128)(2,1)}, u32[]{:S(2)}) copy-start(bf16[256,256]{1,0:T(8,128)(2,1)} %w1_ref.1) | copy-start | bytes 393220
  29.5 70.5 %copy-start.3 = (f32[256]{0:T(256)S(1)}, f32[256]{0:T(256)}, u32[]{:S(2)}) copy-start(f32[256]{0:T(256)} %param.17) | copy-start | bytes 3076
  97.1 12.6 %collective-permute-start = (bf16[256,128]{1,0:T(8,128)(2,1)S(1)}, bf16[256,128]{1,0:T(8,128)(2,1)S(1)}, u32[]{:S(2)}, u32[]{:S(2)}) collective-permute-start(bf16[256,128]{1,0:T(8,128)(2,1)S(1)} %far_sum.1), channel_id=1, source_target_pairs={{0,256},{256,0},{1,257},{257,1},{2,258},{258,2},{3,259},{259,3},{4... | collective-permute-start | bytes 196616 | tf_op jit(solution)/shard_map/ppermute | solution.py:203

commit v5 on v4

--- a/solution.py
+++ b/solution.py
@@ -18,6 +18,17 @@
 META = 8
 LINES = ROWS * FW
 BF, F32 = jnp.bfloat16, jnp.float32
+
+
+def led_by(first, size):
+    order = [first] + [m for m in range(size) if m != first]
+    return order, [order.index(m) for m in range(size)]
+
+
+QUAD_ORDER, QUAD_PLACE = led_by(2 * YS + 2, ZQ * YS)
+FEAT_FIRST = (0 * HS + 1) * XC + 2 * CS + 1
+FEAT_ORDER, FEAT_PLACE = led_by(FEAT_FIRST, QUADS * HS * XC)
+PLANE_ORDER, PLANE_PLACE = led_by(2 * CS + 1, XC)
 VMEM = pl.BlockSpec(memory_space=pltpu.VMEM)
 HBM = pl.BlockSpec(memory_space=pltpu.HBM)
 NT = (((1,), (1,)), ((), ()))
@@ -46,7 +57,7 @@
                 mine = term[i * FW : (i + 1) * FW, i * BLK : (i + 1) * BLK]
                 mine = jnp.where(j + i < count, mine, 0.0).astype(BF)
                 at = (step // ZQ) * MSG + (j + i) * FW
-                out_ref[step % ZQ, y, at : at + FW, :] = mine
+                out_ref[QUAD_PLACE[step % ZQ * YS + y], at : at + FW, :] = mine
 
 
 def first_terms_kernel(
@@ -69,7 +80,7 @@
                 for j in range(CAP):
                     row = rows[0, j, target(r * ZQ + b, y)]
                     place = jnp.where(lane // FW == r * CAP + j, place + row * FW, place)
-            out_ref[b, y, BODY:, :] = place.astype(F32).astype(BF)
+            out_ref[QUAD_PLACE[b * YS + y], BODY:, :] = place.astype(F32).astype(BF)
     for step in range(STEPS):
         if step % WAVE == 0:
             copies[len(small) + step // WAVE].wait()
@@ -109,8 +120,13 @@
 def first_sum_kernel(msg_ref, out_ref):
     for r in range(QUADS):
         total = placed_sum(r, msg_ref, msg_ref).astype(BF)
+        quad = r ^ lax.axis_index("q").astype(jnp.int32)
         for h in range(HS):
-            out_ref[r ^ lax.axis_index("q").astype(jnp.int32), h] = total
+            for e in range(XC):
+                member = (quad * HS + h) * XC + e
+                place = jnp.where(member == FEAT_FIRST, 0, member + (member < FEAT_FIRST).astype(jnp.int32))
+                rows = PLANE_PLACE[e] * 2 * FW
+                out_ref[place] = total[rows : rows + 2 * FW]
 
 
 def far_sum_kernel(msg_ref, meta_ref, out_ref):
@@ -130,16 +146,18 @@
 
 
 def dense_kernel(agg_ref, w1_ref, b1_ref, w2_ref, out_ref):
-    half = agg_ref.shape[0] // 2
-    agg = agg_ref[:half].astype(F32) + agg_ref[half:].astype(F32)
-    agg = jnp.concatenate([agg[:, i * FW : (i + 1) * FW, :].reshape(half * FW, BLK) for i in range(2)], axis=1)
+    half = HS * XC
+    agg = [agg_ref[FEAT_PLACE[m]].astype(F32) + agg_ref[FEAT_PLACE[half + m]].astype(F32) for m in range(half)]
+    agg = [jnp.concatenate([part[i * FW : (i + 1) * FW] for part in agg], axis=0) for i in range(2)]
+    agg = jnp.concatenate(agg, axis=1)
     hidden = lax.dot_general(w1_ref[...], agg.astype(BF), TN, preferred_element_type=F32)
     bias = column(b1_ref)
     hidden = jnp.maximum(hidden + jnp.concatenate([bias, bias], axis=1), 0.0).astype(BF)
     own = pl.multiple_of(lax.axis_index("h").astype(jnp.int32) * (XC * FW), XC * FW)
     out = lax.dot_general(w2_ref[:, pl.ds(own, XC * FW)], hidden, TN, preferred_element_type=F32).astype(BF)
     for i in range(2):
-        out_ref[:, i] = out[:, i * BLK : (i + 1) * BLK].reshape(XC, FW, BLK)
+        for e in range(XC):
+            out_ref[PLANE_PLACE[e], i] = out[e * FW : (e + 1) * FW, i * BLK : (i + 1) * BLK]
 
 
 def call(kernel, name, out_shape, *args, in_specs=None, scratch_shapes=()):
@@ -162,11 +180,10 @@
     copy_sems = pltpu.SemaphoreType.DMA
 
     def message(lines):
-        return jax.ShapeDtypeStruct((ZQ, YS, lines, BLK), BF)
+        return jax.ShapeDtypeStruct((ZQ * YS, lines, BLK), BF)
 
     def quad_exchange(msg):
-        msg = msg.reshape(ZQ * YS, msg.shape[2], BLK)
-        return lax.all_to_all(msg, ("b", "y"), 0, 0, tiled=True)
+        return lax.all_to_all(msg, ("b", "y"), 0, 0, axis_index_groups=[QUAD_ORDER], tiled=True)
 
     msg1, held = call(
         first_terms_kernel,
@@ -181,11 +198,10 @@
         scratch_shapes=[*smem, pltpu.VMEM(features.shape, BF), copy_sems((4 + STEPS // WAVE,))],
     )
     msg1 = quad_exchange(msg1)
-    sums = call(first_sum_kernel, "first_sum", jax.ShapeDtypeStruct((QUADS, HS, LINES, BLK), BF), msg1)
-    sums = sums.reshape(QUADS * HS * XC, 2 * FW, BLK)
-    sums = lax.all_to_all(sums, ("q", "h", "x", "c"), 0, 0, tiled=True)
+    sums = call(first_sum_kernel, "first_sum", jax.ShapeDtypeStruct((QUADS * HS * XC, 2 * FW, BLK), BF), msg1)
+    sums = lax.all_to_all(sums, ("q", "h", "x", "c"), 0, 0, axis_index_groups=[FEAT_ORDER], tiled=True)
     z = call(dense_kernel, "dense", jax.ShapeDtypeStruct((XC, 2, FW, BLK), BF), sums, w1, b1, w2)
-    z = lax.all_to_all(z, ("x", "c"), 0, 0, tiled=True).reshape(ROWS, FW, BLK)
+    z = lax.all_to_all(z, ("x", "c"), 0, 0, axis_index_groups=[PLANE_ORDER], tiled=True).reshape(ROWS, FW, BLK)
 
     msg2 = call(
         second_terms_kernel,

time: 111 us -> 98.9 us (0.89)
  the two profiles are of different devices: /device:TPU:2 before, /device:TPU:8 now
where the time goes in v5:
time: 98.9 us; the launch traced here: 98.6 us
  blocking collectives  78.4 us (79%)
  starting transfers between devices  7.21 us (7%)
  Pallas kernels  7.07 us (7%)
  waiting for transfers between devices  5.21 us (5%)
    all_to_all x2, blocking collectives, quad_exchange(): lax.all_to_all(msg, ('b', 'y'), 0, 0, axis_index_groups=[QUAD_ORDER], til...  40.6 us
    all_to_all x1, blocking collectives, per_device(): lax.all_to_all(sums, ('q', 'h', 'x', 'c'), 0, 0, axis_index_groups=[FEAT_...  30.1 us
    all_to_all x1, blocking collectives, per_device(): lax.all_to_all(z, ('x', 'c'), 0, 0, axis_index_groups=[PLANE_ORDER], tile...  7.68 us
    ppermute x1, starting transfers between devices, per_device(): far = lax.ppermute(far, 'q', [(0, 1), (1, 0)])  7.21 us
    pallas_call x6, Pallas kernels, call(): pl.pallas_call(kernel, in_specs=in_specs or [VMEM] * len(args), out_specs...  7.07 us
    ppermute x1, waiting for transfers between devices, per_device(): far = lax.ppermute(far, 'q', [(0, 1), (1, 0)])  5.21 us
  transfers between devices with their start and end apart: 1, of which 1 were waited for; matrix products, arithmetic and copies ran while one was open for 0% of the time, Pallas kernels for 0%

profile of v5, /device:TPU:8, one launch (start us, length us, event | category | flops | bytes accessed | tf_op | source)
XLA Modules:
  0.0 98.6 jit_solution(17637246109643924017)
XLA Ops:
  0.0 0.0 copy-start.1
  0.0 0.0 copy-start.2
  0.0 0.0 copy-start
  0.0 3.2 %first_terms.1 = (bf16[16,136,128]{2,1,0:T(8,128)(2,1)S(1)}, bf16[8,4,4,128,128]{4,3,2,1,0:T(8,128)(2,1)S(1)}) custom-call(s32[1,4,32]{2,1,0:T(4,128)} %bitcast.11, s32[1,32]{1,0:T(1,128)} %counts_in.3, s32[1,4,32]{2,1,0:T(4,128)} %bitcast.13, bf16[16,16,128]{2,1,0:T(8,128)(2,1)} %values_in.1, bf16[1,8,4,4,128,128]{5,4,3,2,1,0:T(8,128)(2,1)} %bitcast.10), custom_call_target="tpu_custom_call" | custom-call | tf_op jit(solution)/shard_map/first_terms/pallas_call | solution.py:164
  3.3 22.3 %all_to_all.20.msg_ref.meta_ref = bf16[16,136,128]{2,1,0:T(8,128)(2,1)S(1)} all-to-all(bf16[16,136,128]{2,1,0:T(8,128)(2,1)S(1)} %get-tuple-element.7), channel_id=1, replica_groups={{160,0,16,32,48,64,80,96,112,128,144,176,192,208,224,240},{161,1,17,33,..., dimensions={0} | all-to-all | bytes 1114112 | tf_op jit(solution)/shard_map/all_to_all | solution.py:186
  25.6 0.5 first_sum.1
  26.0 0.0 copy-start.3
  26.1 30.1 %all_to_all.21.agg_ref = bf16[32,32,128]{2,1,0:T(8,128)(2,1)S(1)} all-to-all(bf16[32,32,128]{2,1,0:T(8,128)(2,1)S(1)} %first_sum.1), channel_id=1, replica_groups={{13,0,1,2,3,4,5,6,7,8,9,10,11,12,14,15,256,257,258,259,260,261,262,263,..., dimensions={0} | all-to-all | bytes 524288 | tf_op jit(solution)/shard_map/all_to_all | solution.py:202
  56.2 0.0 copy-done.1
  56.2 0.0 copy-done.2
  56.2 0.0 copy-done
  56.2 0.4 dense.1
  56.6 7.7 %all_to_all.22 = bf16[8,2,16,128]{3,2,1,0:T(8,128)(2,1)S(1)} all-to-all(bf16[8,2,16,128]{3,2,1,0:T(8,128)(2,1)S(1)} %dense.1), channel_id=1, replica_groups={{5,0,1,2,3,4,6,7},{13,8,9,10,11,12,14,15},{21,16,17,18,19,20,22,23},{29..., dimensions={0} | all-to-all | bytes 131072 | tf_op jit(solution)/shard_map/all_to_all | solution.py:204
  64.3 2.3 %second_terms.1 = bf16[16,128,128]{2,1,0:T(8,128)(2,1)S(1)} custom-call(s32[1,4,32]{2,1,0:T(4,128)} %bitcast.12, s32[1,32]{1,0:T(1,128)} %counts_in.3, bf16[16,16,128]{2,1,0:T(8,128)(2,1)S(1)} %bitcast.7, bf16[8,4,4,128,128]{4,3,2,1,0:T(8,128)(2,1)S(1)} %get-tuple-element.8.tiles_ref), custom_call_target="tpu_custom_call" | custom-call | tf_op jit(solution)/shard_map/second_terms/pallas_call | solution.py:164
  66.5 18.3 %all_to_all.23.msg_ref = bf16[16,128,128]{2,1,0:T(8,128)(2,1)S(1)} all-to-all(bf16[16,128,128]{2,1,0:T(8,128)(2,1)S(1)} %second_terms.1), channel_id=1, replica_groups={{160,0,16,32,48,64,80,96,112,128,144,176,192,208,224,240},{161,1,17,33,..., dimensions={0} | all-to-all | bytes 1048576 | tf_op jit(solution)/shard_map/all_to_all | solution.py:186
  84.8 0.3 far_sum.1
  85.2 7.2 %collective-permute-start = (bf16[256,128]{1,0:T(8,128)(2,1)S(1)}, bf16[256,128]{1,0:T(8,128)(2,1)S(1)}, u32[]{:S(2)}, u32[]{:S(2)}) collective-permute-start(bf16[256,128]{1,0:T(8,128)(2,1)S(1)} %far_sum.1), channel_id=1, source_target_pairs={{0,256},{256,0},{1,257},{257,1},{2,258},{258,2},{3,259},{259,3},{4... | collective-permute-start | bytes 196616 | tf_op jit(solution)/shard_map/ppermute | solution.py:219
  92.4 0.0 copy-done.3
  92.4 0.4 near_sum.1
  92.8 5.2 %collective-permute-done = bf16[256,128]{1,0:T(8,128)(2,1)S(1)} collective-permute-done((bf16[256,128]{1,0:T(8,128)(2,1)S(1)}, bf16[256,128]{1,0:T(8,128)(2,1)S(1)}, u32[]{:S(2)}, u32[]{:S(2)}) %collective-permute-start) | collective-permute-done | bytes 65568 | tf_op jit(solution)/shard_map/ppermute | solution.py:219
  98.0 0.7 convert_add_fusion
Async XLA Ops:
  0.0 56.2 %copy-start.1 = (bf16[256,256]{1,0:T(8,128)(2,1)S(1)}, bf16[256,256]{1,0:T(8,128)(2,1)}, u32[]{:S(2)}) copy-start(bf16[256,256]{1,0:T(8,128)(2,1)} %w2_ref.1) | copy-start | bytes 393220
  0.0 56.2 %copy-start.2 = (f32[256]{0:T(256)S(1)}, f32[256]{0:T(256)}, u32[]{:S(2)}) copy-start(f32[256]{0:T(256)} %param.15) | copy-start | bytes 3076
  0.0 56.2 %copy-start = (bf16[256,256]{1,0:T(8,128)(2,1)S(1)}, bf16[256,256]{1,0:T(8,128)(2,1)}, u32[]{:S(2)}) copy-start(bf16[256,256]{1,0:T(8,128)(2,1)} %w1_ref.1) | copy-start | bytes 393220
  26.0 66.3 %copy-start.3 = (f32[256]{0:T(256)S(1)}, f32[256]{0:T(256)}, u32[]{:S(2)}) copy-start(f32[256]{0:T(256)} %param.17) | copy-start | bytes 3076
  85.2 12.8 %collective-permute-start = (bf16[256,128]{1,0:T(8,128)(2,1)S(1)}, bf16[256,128]{1,0:T(8,128)(2,1)S(1)}, u32[]{:S(2)}, u32[]{:S(2)}) collective-permute-start(bf16[256,128]{1,0:T(8,128)(2,1)S(1)} %far_sum.1), channel_id=1, source_target_pairs={{0,256},{256,0},{1,257},{257,1},{2,258},{258,2},{3,259},{259,3},{4... | collective-permute-start | bytes 196616 | tf_op jit(solution)/shard_map/ppermute | solution.py:219

commit v6 on v5

--- a/solution.py
+++ b/solution.py
@@ -25,7 +25,7 @@
     return order, [order.index(m) for m in range(size)]
 
 
-QUAD_ORDER, QUAD_PLACE = led_by(2 * YS + 2, ZQ * YS)
+QUAD_ORDER, QUAD_PLACE = led_by(1 * YS + 2, ZQ * YS)
 FEAT_FIRST = (0 * HS + 1) * XC + 2 * CS + 1
 FEAT_ORDER, FEAT_PLACE = led_by(FEAT_FIRST, QUADS * HS * XC)
 PLANE_ORDER, PLANE_PLACE = led_by(2 * CS + 1, XC)

time: 98.9 us -> 98.3 us (level)
  the two profiles are of different devices: /device:TPU:8 before, /device:TPU:2 now
where the time goes in v6:
time: 98.3 us; the launch traced here: 98 us
  blocking collectives  78.3 us (80%)
  starting transfers between devices  7.25 us (7%)
  Pallas kernels  7.08 us (7%)
  waiting for transfers between devices  4.54 us (5%)
    all_to_all x2, blocking collectives, quad_exchange(): lax.all_to_all(msg, ('b', 'y'), 0, 0, axis_index_groups=[QUAD_ORDER], til...  41.7 us
    all_to_all x1, blocking collectives, per_device(): lax.all_to_all(sums, ('q', 'h', 'x', 'c'), 0, 0, axis_index_groups=[FEAT_...  29.1 us
    all_to_all x1, blocking collectives, per_device(): lax.all_to_all(z, ('x', 'c'), 0, 0, axis_index_groups=[PLANE_ORDER], tile...  7.59 us
    ppermute x1, starting transfers between devices, per_device(): far = lax.ppermute(far, 'q', [(0, 1), (1, 0)])  7.25 us
    pallas_call x6, Pallas kernels, call(): pl.pallas_call(kernel, in_specs=in_specs or [VMEM] * len(args), out_specs...  7.08 us
    ppermute x1, waiting for transfers between devices, per_device(): far = lax.ppermute(far, 'q', [(0, 1), (1, 0)])  4.54 us
  transfers between devices with their start and end apart: 1, of which 1 were waited for; matrix products, arithmetic and copies ran while one was open for 0% of the time, Pallas kernels for 0%

profile of v6, /device:TPU:2, one launch (start us, length us, event | category | flops | bytes accessed | tf_op | source)
XLA Modules:
  0.0 98.0 jit_solution(9221569089352951378)
XLA Ops:
  0.0 0.0 copy-start.1
  0.0 0.0 copy-start.2
  0.0 0.0 copy-start
  0.0 3.2 %first_terms.1 = (bf16[16,136,128]{2,1,0:T(8,128)(2,1)S(1)}, bf16[8,4,4,128,128]{4,3,2,1,0:T(8,128)(2,1)S(1)}) custom-call(s32[1,4,32]{2,1,0:T(4,128)} %bitcast.11, s32[1,32]{1,0:T(1,128)} %counts_in.3, s32[1,4,32]{2,1,0:T(4,128)} %bitcast.13, bf16[16,16,128]{2,1,0:T(8,128)(2,1)} %values_in.1, bf16[1,8,4,4,128,128]{5,4,3,2,1,0:T(8,128)(2,1)} %bitcast.10), custom_call_target="tpu_custom_call" | custom-call | tf_op jit(solution)/shard_map/first_terms/pallas_call | solution.py:164
  3.3 23.3 %all_to_all.20.msg_ref.meta_ref = bf16[16,136,128]{2,1,0:T(8,128)(2,1)S(1)} all-to-all(bf16[16,136,128]{2,1,0:T(8,128)(2,1)S(1)} %get-tuple-element.7), channel_id=1, replica_groups={{96,0,16,32,48,64,80,112,128,144,160,176,192,208,224,240},{97,1,17,33,4..., dimensions={0} | all-to-all | bytes 1114112 | tf_op jit(solution)/shard_map/all_to_all | solution.py:186
  26.6 0.5 first_sum.1
  27.1 0.0 copy-start.3
  27.1 29.1 %all_to_all.21.agg_ref = bf16[32,32,128]{2,1,0:T(8,128)(2,1)S(1)} all-to-all(bf16[32,32,128]{2,1,0:T(8,128)(2,1)S(1)} %first_sum.1), channel_id=1, replica_groups={{13,0,1,2,3,4,5,6,7,8,9,10,11,12,14,15,256,257,258,259,260,261,262,263,..., dimensions={0} | all-to-all | bytes 524288 | tf_op jit(solution)/shard_map/all_to_all | solution.py:202
  56.2 0.0 copy-done.1
  56.2 0.0 copy-done.2
  56.2 0.0 copy-done
  56.2 0.4 dense.1
  56.6 7.6 %all_to_all.22 = bf16[8,2,16,128]{3,2,1,0:T(8,128)(2,1)S(1)} all-to-all(bf16[8,2,16,128]{3,2,1,0:T(8,128)(2,1)S(1)} %dense.1), channel_id=1, replica_groups={{5,0,1,2,3,4,6,7},{13,8,9,10,11,12,14,15},{21,16,17,18,19,20,22,23},{29..., dimensions={0} | all-to-all | bytes 131072 | tf_op jit(solution)/shard_map/all_to_all | solution.py:204
  64.2 2.3 %second_terms.1 = bf16[16,128,128]{2,1,0:T(8,128)(2,1)S(1)} custom-call(s32[1,4,32]{2,1,0:T(4,128)} %bitcast.12, s32[1,32]{1,0:T(1,128)} %counts_in.3, bf16[16,16,128]{2,1,0:T(8,128)(2,1)S(1)} %bitcast.7, bf16[8,4,4,128,128]{4,3,2,1,0:T(8,128)(2,1)S(1)} %get-tuple-element.8.tiles_ref), custom_call_target="tpu_custom_call" | custom-call | tf_op jit(solution)/shard_map/second_terms/pallas_call | solution.py:164
  66.4 18.3 %all_to_all.23.msg_ref = bf16[16,128,128]{2,1,0:T(8,128)(2,1)S(1)} all-to-all(bf16[16,128,128]{2,1,0:T(8,128)(2,1)S(1)} %second_terms.1), channel_id=1, replica_groups={{96,0,16,32,48,64,80,112,128,144,160,176,192,208,224,240},{97,1,17,33,4..., dimensions={0} | all-to-all | bytes 1048576 | tf_op jit(solution)/shard_map/all_to_all | solution.py:186
  84.8 0.3 far_sum.1
  85.1 7.2 %collective-permute-start = (bf16[256,128]{1,0:T(8,128)(2,1)S(1)}, bf16[256,128]{1,0:T(8,128)(2,1)S(1)}, u32[]{:S(2)}, u32[]{:S(2)}) collective-permute-start(bf16[256,128]{1,0:T(8,128)(2,1)S(1)} %far_sum.1), channel_id=1, source_target_pairs={{0,256},{256,0},{1,257},{257,1},{2,258},{258,2},{3,259},{259,3},{4... | collective-permute-start | bytes 196616 | tf_op jit(solution)/shard_map/ppermute | solution.py:219
  92.4 0.0 copy-done.3
  92.4 0.4 near_sum.1
  92.8 4.5 %collective-permute-done = bf16[256,128]{1,0:T(8,128)(2,1)S(1)} collective-permute-done((bf16[256,128]{1,0:T(8,128)(2,1)S(1)}, bf16[256,128]{1,0:T(8,128)(2,1)S(1)}, u32[]{:S(2)}, u32[]{:S(2)}) %collective-permute-start) | collective-permute-done | bytes 65568 | tf_op jit(solution)/shard_map/ppermute | solution.py:219
  97.3 0.7 convert_add_fusion
Async XLA Ops:
  0.0 56.2 %copy-start.1 = (bf16[256,256]{1,0:T(8,128)(2,1)S(1)}, bf16[256,256]{1,0:T(8,128)(2,1)}, u32[]{:S(2)}) copy-start(bf16[256,256]{1,0:T(8,128)(2,1)} %w2_ref.1) | copy-start | bytes 393220
  0.0 56.2 %copy-start.2 = (f32[256]{0:T(256)S(1)}, f32[256]{0:T(256)}, u32[]{:S(2)}) copy-start(f32[256]{0:T(256)} %param.15) | copy-start | bytes 3076
  0.0 56.2 %copy-start = (bf16[256,256]{1,0:T(8,128)(2,1)S(1)}, bf16[256,256]{1,0:T(8,128)(2,1)}, u32[]{:S(2)}) copy-start(bf16[256,256]{1,0:T(8,128)(2,1)} %w1_ref.1) | copy-start | bytes 393220
  27.1 65.3 %copy-start.3 = (f32[256]{0:T(256)S(1)}, f32[256]{0:T(256)}, u32[]{:S(2)}) copy-start(f32[256]{0:T(256)} %param.17) | copy-start | bytes 3076
  85.1 12.2 %collective-permute-start = (bf16[256,128]{1,0:T(8,128)(2,1)S(1)}, bf16[256,128]{1,0:T(8,128)(2,1)S(1)}, u32[]{:S(2)}, u32[]{:S(2)}) collective-permute-start(bf16[256,128]{1,0:T(8,128)(2,1)S(1)} %far_sum.1), channel_id=1, source_target_pairs={{0,256},{256,0},{1,257},{257,1},{2,258},{258,2},{3,259},{259,3},{4... | collective-permute-start | bytes 196616 | tf_op jit(solution)/shard_map/ppermute | solution.py:219

commit v7 on v6

--- a/solution.py
+++ b/solution.py
@@ -61,7 +61,7 @@
 
 
 def first_terms_kernel(
-    cols_in, counts_in, rows_in, values_in, tiles_in, out_ref, tiles_ref, cols, counts, rows, values, sems
+    cols_in, counts_in, rows_in, values_in, tiles_in, out_ref, tiles_ref, pick_ref, cols, counts, rows, values, sems
 ):
     small = list(zip((cols_in, counts_in, rows_in, values_in), (cols, counts, rows, values)))
     copies = [pltpu.make_async_copy(src, dst, sems.at[i]) for i, (src, dst) in enumerate(small)]
@@ -81,20 +81,36 @@
                     row = rows[0, j, target(r * ZQ + b, y)]
                     place = jnp.where(lane // FW == r * CAP + j, place + row * FW, place)
             out_ref[QUAD_PLACE[b * YS + y], BODY:, :] = place.astype(F32).astype(BF)
+    shape = (FW, LINES)
+    gap = lax.broadcasted_iota(jnp.int32, shape, 1) - lax.broadcasted_iota(jnp.int32, shape, 0)
+    for step in range(STEPS):
+        for y in range(YS):
+            p = target(step, y)
+            for j in range(CAP):
+                start = jnp.where(j < counts[0, p], cols[0, j, p] * FW, -LINES)
+                at = ((step * YS + y) * CAP + j) * FW
+                pick_ref[at : at + FW, :] = jnp.where(gap == start, 1.0, 0.0).astype(BF)
     for step in range(STEPS):
         if step % WAVE == 0:
             copies[len(small) + step // WAVE].wait()
         write_terms(step, cols, counts, values, tiles_ref, out_ref)
 
 
-def second_terms_kernel(cols_in, counts_in, values_ref, tiles_ref, out_ref, cols, counts, sems):
-    copies = [pltpu.make_async_copy(cols_in, cols, sems.at[0]), pltpu.make_async_copy(counts_in, counts, sems.at[1])]
-    for copy in copies:
-        copy.start()
-    for copy in copies:
-        copy.wait()
+def second_terms_kernel(pick_ref, values_ref, tiles_ref, out_ref):
+    values = values_ref[...].reshape(LINES, BLK)
+    lines = YS * MSG
     for step in range(STEPS):
-        write_terms(step, cols, counts, values_ref, tiles_ref, out_ref)
+        pick = pick_ref[step * lines : (step + 1) * lines, :]
+        picked = jnp.dot(pick, values, preferred_element_type=F32).astype(BF)
+        for y in range(YS):
+            for j in range(0, CAP, 2):
+                at = y * MSG + j * FW
+                tiles = tiles_ref[step, y, j : j + 2].reshape(2 * BLK, BLK)
+                term = lax.dot_general(picked[at : at + 2 * FW], tiles, NT, preferred_element_type=F32).astype(BF)
+                for i in range(2):
+                    mine = term[i * FW : (i + 1) * FW, i * BLK : (i + 1) * BLK]
+                    to = (step // ZQ) * MSG + (j + i) * FW
+                    out_ref[QUAD_PLACE[step % ZQ * YS + y], to : to + FW, :] = mine
 
 
 def placed_sum(r, msg_ref, meta_ref):
@@ -185,10 +201,10 @@
     def quad_exchange(msg):
         return lax.all_to_all(msg, ("b", "y"), 0, 0, axis_index_groups=[QUAD_ORDER], tiled=True)
 
-    msg1, held = call(
+    msg1, held, pick = call(
         first_terms_kernel,
         "first_terms",
-        (message(BODY + META), pltpu.VMEM((STEPS, YS, CAP, BLK, BLK), BF)),
+        (message(BODY + META), pltpu.VMEM((STEPS, YS, CAP, BLK, BLK), BF), pltpu.VMEM((STEPS * YS * MSG, LINES), BF)),
         cols,
         counts,
         rows,
@@ -203,17 +219,7 @@
     z = call(dense_kernel, "dense", jax.ShapeDtypeStruct((XC, 2, FW, BLK), BF), sums, w1, b1, w2)
     z = lax.all_to_all(z, ("x", "c"), 0, 0, axis_index_groups=[PLANE_ORDER], tiled=True).reshape(ROWS, FW, BLK)
 
-    msg2 = call(
-        second_terms_kernel,
-        "second_terms",
-        message(BODY),
-        cols,
-        counts,
-        z,
-        held,
-        in_specs=[HBM, HBM, VMEM, VMEM],
-        scratch_shapes=[*smem[:2], copy_sems((2,))],
-    )
+    msg2 = call(second_terms_kernel, "second_terms", message(BODY), pick, z, held)
     msg2 = quad_exchange(msg2)
     far = call(far_sum_kernel, "far_sum", jax.ShapeDtypeStruct((LINES, BLK), BF), msg2, msg1)
     far = lax.ppermute(far, "q", [(0, 1), (1, 0)])

time: 98.3 us -> 98.4 us (level)
  the two profiles are of different devices: /device:TPU:2 before, /device:TPU:8 now
where the time goes in v7:
time: 98.4 us; the launch traced here: 98.1 us
  blocking collectives  78.6 us (80%)
  starting transfers between devices  6.96 us (7%)
  Pallas kernels  6.9 us (7%)
  waiting for transfers between devices  4.91 us (5%)
    all_to_all x2, blocking collectives, quad_exchange(): lax.all_to_all(msg, ('b', 'y'), 0, 0, axis_index_groups=[QUAD_ORDER], til...  41.2 us
    all_to_all x1, blocking collectives, per_device(): lax.all_to_all(sums, ('q', 'h', 'x', 'c'), 0, 0, axis_index_groups=[FEAT_...  29.8 us
    all_to_all x1, blocking collectives, per_device(): lax.all_to_all(z, ('x', 'c'), 0, 0, axis_index_groups=[PLANE_ORDER], tile...  7.51 us
    ppermute x1, starting transfers between devices, per_device(): far = lax.ppermute(far, 'q', [(0, 1), (1, 0)])  6.96 us
    pallas_call x6, Pallas kernels, call(): pl.pallas_call(kernel, in_specs=in_specs or [VMEM] * len(args), out_specs...  6.9 us
    ppermute x1, waiting for transfers between devices, per_device(): far = lax.ppermute(far, 'q', [(0, 1), (1, 0)])  4.91 us
  transfers between devices with their start and end apart: 1, of which 1 were waited for; matrix products, arithmetic and copies ran while one was open for 0% of the time, Pallas kernels for 0%

profile of v7, /device:TPU:8, one launch (start us, length us, event | category | flops | bytes accessed | tf_op | source)
XLA Modules:
  0.0 98.1 jit_solution(10719578872788456106)
XLA Ops:
  0.0 0.0 copy-start.1
  0.0 0.0 copy-start.2
  0.0 0.0 copy-start
  0.0 3.2 %first_terms.1 = (bf16[16,136,128]{2,1,0:T(8,128)(2,1)S(1)}, bf16[8,4,4,128,128]{4,3,2,1,0:T(8,128)(2,1)S(1)}, bf16[2048,256]{1,0:T(8,128)(2,1)S(1)}) custom-call(s32[1,4,32]{2,1,0:T(4,128)} %bitcast.11, s32[1,32]{1,0:T(1,128)} %counts_in.1, s32[1,4,32]{2,1,0:T(4,128)} %bitcast.12, bf16[16,16,128]{2,1,0:T(8,128)(2,1)} %values_in.1, ...), custom_call_target="tpu_custom_call" | custom-call | tf_op jit(solution)/shard_map/first_terms/pallas_call | solution.py:180
  3.3 23.1 %all_to_all.20.msg_ref.meta_ref = bf16[16,136,128]{2,1,0:T(8,128)(2,1)S(1)} all-to-all(bf16[16,136,128]{2,1,0:T(8,128)(2,1)S(1)} %get-tuple-element.9), channel_id=1, replica_groups={{96,0,16,32,48,64,80,112,128,144,160,176,192,208,224,240},{97,1,17,33,4..., dimensions={0} | all-to-all | bytes 1114112 | tf_op jit(solution)/shard_map/all_to_all | solution.py:202
  26.4 0.5 first_sum.1
  26.8 29.8 %all_to_all.21.agg_ref = bf16[32,32,128]{2,1,0:T(8,128)(2,1)S(1)} all-to-all(bf16[32,32,128]{2,1,0:T(8,128)(2,1)S(1)} %first_sum.1), channel_id=1, replica_groups={{13,0,1,2,3,4,5,6,7,8,9,10,11,12,14,15,256,257,258,259,260,261,262,263,..., dimensions={0} | all-to-all | bytes 524288 | tf_op jit(solution)/shard_map/all_to_all | solution.py:218
  56.7 0.0 copy-done.1
  56.7 0.0 copy-done.2
  56.7 0.0 copy-done
  56.7 0.4 dense.1
  57.1 0.0 copy-start.3
  57.1 7.5 %all_to_all.22 = bf16[8,2,16,128]{3,2,1,0:T(8,128)(2,1)S(1)} all-to-all(bf16[8,2,16,128]{3,2,1,0:T(8,128)(2,1)S(1)} %dense.1), channel_id=1, replica_groups={{5,0,1,2,3,4,6,7},{13,8,9,10,11,12,14,15},{21,16,17,18,19,20,22,23},{29..., dimensions={0} | all-to-all | bytes 131072 | tf_op jit(solution)/shard_map/all_to_all | solution.py:220
  64.6 2.1 %second_terms.1 = bf16[16,128,128]{2,1,0:T(8,128)(2,1)S(1)} custom-call(bf16[2048,256]{1,0:T(8,128)(2,1)S(1)} %get-tuple-element.8.pick_ref, bf16[16,16,128]{2,1,0:T(8,128)(2,1)S(1)} %bitcast.7, bf16[8,4,4,128,128]{4,3,2,1,0:T(8,128)(2,1)S(1)} %get-tuple-element.10.tiles_ref), custom_call_target="tpu_custom_call" | custom-call | tf_op jit(solution)/shard_map/second_terms/pallas_call | solution.py:180
  66.7 18.1 %all_to_all.23.msg_ref = bf16[16,128,128]{2,1,0:T(8,128)(2,1)S(1)} all-to-all(bf16[16,128,128]{2,1,0:T(8,128)(2,1)S(1)} %second_terms.1), channel_id=1, replica_groups={{96,0,16,32,48,64,80,112,128,144,160,176,192,208,224,240},{97,1,17,33,4..., dimensions={0} | all-to-all | bytes 1048576 | tf_op jit(solution)/shard_map/all_to_all | solution.py:202
  84.8 0.3 far_sum.1
  85.2 7.0 %collective-permute-start = (bf16[256,128]{1,0:T(8,128)(2,1)S(1)}, bf16[256,128]{1,0:T(8,128)(2,1)S(1)}, u32[]{:S(2)}, u32[]{:S(2)}) collective-permute-start(bf16[256,128]{1,0:T(8,128)(2,1)S(1)} %far_sum.1), channel_id=1, source_target_pairs={{0,256},{256,0},{1,257},{257,1},{2,258},{258,2},{3,259},{259,3},{4... | collective-permute-start | bytes 196616 | tf_op jit(solution)/shard_map/ppermute | solution.py:225
  92.1 0.0 copy-done.3
  92.2 0.4 near_sum.1
  92.5 4.9 %collective-permute-done = bf16[256,128]{1,0:T(8,128)(2,1)S(1)} collective-permute-done((bf16[256,128]{1,0:T(8,128)(2,1)S(1)}, bf16[256,128]{1,0:T(8,128)(2,1)S(1)}, u32[]{:S(2)}, u32[]{:S(2)}) %collective-permute-start) | collective-permute-done | bytes 65568 | tf_op jit(solution)/shard_map/ppermute | solution.py:225
  97.4 0.7 convert_add_fusion
Async XLA Ops:
  0.0 56.7 %copy-start.1 = (bf16[256,256]{1,0:T(8,128)(2,1)S(1)}, bf16[256,256]{1,0:T(8,128)(2,1)}, u32[]{:S(2)}) copy-start(bf16[256,256]{1,0:T(8,128)(2,1)} %w2_ref.1) | copy-start | bytes 393220
  0.0 56.7 %copy-start.2 = (f32[256]{0:T(256)S(1)}, f32[256]{0:T(256)}, u32[]{:S(2)}) copy-start(f32[256]{0:T(256)} %param.15) | copy-start | bytes 3076
  0.0 56.7 %copy-start = (bf16[256,256]{1,0:T(8,128)(2,1)S(1)}, bf16[256,256]{1,0:T(8,128)(2,1)}, u32[]{:S(2)}) copy-start(bf16[256,256]{1,0:T(8,128)(2,1)} %w1_ref.1) | copy-start | bytes 393220
  57.1 35.0 %copy-start.3 = (f32[256]{0:T(256)S(1)}, f32[256]{0:T(256)}, u32[]{:S(2)}) copy-start(f32[256]{0:T(256)} %param.17) | copy-start | bytes 3076
  85.2 12.3 %collective-permute-start = (bf16[256,128]{1,0:T(8,128)(2,1)S(1)}, bf16[256,128]{1,0:T(8,128)(2,1)S(1)}, u32[]{:S(2)}, u32[]{:S(2)}) collective-permute-start(bf16[256,128]{1,0:T(8,128)(2,1)S(1)} %far_sum.1), channel_id=1, source_target_pairs={{0,256},{256,0},{1,257},{257,1},{2,258},{258,2},{3,259},{259,3},{4... | collective-permute-start | bytes 196616 | tf_op jit(solution)/shard_map/ppermute | solution.py:225

commit v8 on v6

--- a/solution.py
+++ b/solution.py
@@ -20,15 +20,32 @@
 BF, F32 = jnp.bfloat16, jnp.float32
 
 
-def led_by(first, size):
-    order = [first] + [m for m in range(size) if m != first]
+def led_by(first, size, hops):
+    order = [first] + sorted((m for m in range(size) if m != first), key=lambda m: -hops(m, first))
     return order, [order.index(m) for m in range(size)]
 
 
-QUAD_ORDER, QUAD_PLACE = led_by(1 * YS + 2, ZQ * YS)
+def ring(a, b, size):
+    return min((a - b) % size, (b - a) % size)
+
+
+def quad_hops(m, n):
+    return abs(m // YS - n // YS) + ring(m % YS, n % YS, YS)
+
+
+def plane_hops(m, n):
+    return ring(m // CS, n // CS, XS) + (m % CS != n % CS)
+
+
+def feat_hops(m, n):
+    z, w = ((k // XC % HS) * QUADS + k // XC // HS for k in (m, n))
+    return ZQ * ring(z, w, QUADS * HS) + plane_hops(m % XC, n % XC)
+
+
+QUAD_ORDER, QUAD_PLACE = led_by(1 * YS + 2, ZQ * YS, quad_hops)
 FEAT_FIRST = (0 * HS + 1) * XC + 2 * CS + 1
-FEAT_ORDER, FEAT_PLACE = led_by(FEAT_FIRST, QUADS * HS * XC)
-PLANE_ORDER, PLANE_PLACE = led_by(2 * CS + 1, XC)
+FEAT_ORDER, FEAT_PLACE = led_by(FEAT_FIRST, QUADS * HS * XC, feat_hops)
+PLANE_ORDER, PLANE_PLACE = led_by(2 * CS + 1, XC, plane_hops)
 VMEM = pl.BlockSpec(memory_space=pltpu.VMEM)
 HBM = pl.BlockSpec(memory_space=pltpu.HBM)
 NT = (((1,), (1,)), ((), ()))
@@ -123,8 +140,8 @@
         quad = r ^ lax.axis_index("q").astype(jnp.int32)
         for h in range(HS):
             for e in range(XC):
-                member = (quad * HS + h) * XC + e
-                place = jnp.where(member == FEAT_FIRST, 0, member + (member < FEAT_FIRST).astype(jnp.int32))
+                member = h * XC + e
+                place = jnp.where(quad == 0, FEAT_PLACE[member], FEAT_PLACE[HS * XC + member])
                 rows = PLANE_PLACE[e] * 2 * FW
                 out_ref[place] = total[rows : rows + 2 * FW]
 

time: 98.3 us -> 99.1 us (level)
  blocking collectives: 78.3 us -> 79.9 us
    all_to_all x2, blocking collectives: 41.7 us -> 43.2 us  [quad_exchange(): lax.all_to_all(msg, ('b', 'y'), 0, 0, axis_index_groups=[QUAD_ORDER], til...]
where the time goes in v8:
time: 99.1 us; the launch traced here: 98.8 us
  blocking collectives  79.9 us (81%)
  starting transfers between devices  7.3 us (7%)
  Pallas kernels  7.09 us (7%)
  waiting for transfers between devices  3.78 us (4%)
    all_to_all x2, blocking collectives, quad_exchange(): lax.all_to_all(msg, ('b', 'y'), 0, 0, axis_index_groups=[QUAD_ORDER], til...  43.2 us
    all_to_all x1, blocking collectives, per_device(): lax.all_to_all(sums, ('q', 'h', 'x', 'c'), 0, 0, axis_index_groups=[FEAT_...  29.8 us
    ppermute x1, starting transfers between devices, per_device(): far = lax.ppermute(far, 'q', [(0, 1), (1, 0)])  7.3 us
    pallas_call x6, Pallas kernels, call(): pl.pallas_call(kernel, in_specs=in_specs or [VMEM] * len(args), out_specs...  7.09 us
    all_to_all x1, blocking collectives, per_device(): lax.all_to_all(z, ('x', 'c'), 0, 0, axis_index_groups=[PLANE_ORDER], tile...  6.97 us
    ppermute x1, waiting for transfers between devices, per_device(): far = lax.ppermute(far, 'q', [(0, 1), (1, 0)])  3.78 us
  transfers between devices with their start and end apart: 1, of which 1 were waited for; matrix products, arithmetic and copies ran while one was open for 0% of the time, Pallas kernels for 0%

profile of v8, /device:TPU:2, one launch (start us, length us, event | category | flops | bytes accessed | tf_op | source)
XLA Modules:
  0.0 98.8 jit_solution(3046244545639820852)
XLA Ops:
  0.0 0.0 copy-start.1
  0.0 0.0 copy-start.2
  0.0 0.0 copy-start
  0.0 3.2 %first_terms.1 = (bf16[16,136,128]{2,1,0:T(8,128)(2,1)S(1)}, bf16[8,4,4,128,128]{4,3,2,1,0:T(8,128)(2,1)S(1)}) custom-call(s32[1,4,32]{2,1,0:T(4,128)} %bitcast.11, s32[1,32]{1,0:T(1,128)} %counts_in.3, s32[1,4,32]{2,1,0:T(4,128)} %bitcast.13, bf16[16,16,128]{2,1,0:T(8,128)(2,1)} %values_in.1, bf16[1,8,4,4,128,128]{5,4,3,2,1,0:T(8,128)(2,1)} %bitcast.10), custom_call_target="tpu_custom_call" | custom-call | tf_op jit(solution)/shard_map/first_terms/pallas_call | solution.py:181
  3.3 23.3 %all_to_all.20.msg_ref.meta_ref = bf16[16,136,128]{2,1,0:T(8,128)(2,1)S(1)} all-to-all(bf16[16,136,128]{2,1,0:T(8,128)(2,1)S(1)} %get-tuple-element.7), channel_id=1, replica_groups={{96,192,0,128,208,240,16,48,64,144,176,224,32,80,112,160},{97,193,1,129..., dimensions={0} | all-to-all | bytes 1114112 | tf_op jit(solution)/shard_map/all_to_all | solution.py:203
  26.6 0.5 first_sum.1
  27.1 0.0 copy-start.3
  27.1 29.8 %all_to_all.21.agg_ref = bf16[32,32,128]{2,1,0:T(8,128)(2,1)S(1)} all-to-all(bf16[32,32,128]{2,1,0:T(8,128)(2,1)S(1)} %first_sum.1), channel_id=1, replica_groups={{13,0,1,2,6,3,4,7,5,256,264,257,258,262,265,266,270,259,260,263,267,268..., dimensions={0} | all-to-all | bytes 524288 | tf_op jit(solution)/shard_map/all_to_all | solution.py:219
  56.9 0.0 copy-done.1
  56.9 0.0 copy-done.2
  56.9 0.0 copy-done
  56.9 0.4 dense.1
  57.3 7.0 %all_to_all.22 = bf16[8,2,16,128]{3,2,1,0:T(8,128)(2,1)S(1)} all-to-all(bf16[8,2,16,128]{3,2,1,0:T(8,128)(2,1)S(1)} %dense.1), channel_id=1, replica_groups={{5,0,1,2,6,3,4,7},{13,8,9,10,14,11,12,15},{21,16,17,18,22,19,20,23},{29..., dimensions={0} | all-to-all | bytes 131072 | tf_op jit(solution)/shard_map/all_to_all | solution.py:221
  64.2 2.3 %second_terms.1 = bf16[16,128,128]{2,1,0:T(8,128)(2,1)S(1)} custom-call(s32[1,4,32]{2,1,0:T(4,128)} %bitcast.12, s32[1,32]{1,0:T(1,128)} %counts_in.3, bf16[16,16,128]{2,1,0:T(8,128)(2,1)S(1)} %bitcast.7, bf16[8,4,4,128,128]{4,3,2,1,0:T(8,128)(2,1)S(1)} %get-tuple-element.8.tiles_ref), custom_call_target="tpu_custom_call" | custom-call | tf_op jit(solution)/shard_map/second_terms/pallas_call | solution.py:181
  66.5 19.8 %all_to_all.23.msg_ref = bf16[16,128,128]{2,1,0:T(8,128)(2,1)S(1)} all-to-all(bf16[16,128,128]{2,1,0:T(8,128)(2,1)S(1)} %second_terms.1), channel_id=1, replica_groups={{96,192,0,128,208,240,16,48,64,144,176,224,32,80,112,160},{97,193,1,129..., dimensions={0} | all-to-all | bytes 1048576 | tf_op jit(solution)/shard_map/all_to_all | solution.py:203
  86.3 0.4 far_sum.1
  86.7 7.3 %collective-permute-start = (bf16[256,128]{1,0:T(8,128)(2,1)S(1)}, bf16[256,128]{1,0:T(8,128)(2,1)S(1)}, u32[]{:S(2)}, u32[]{:S(2)}) collective-permute-start(bf16[256,128]{1,0:T(8,128)(2,1)S(1)} %far_sum.1), channel_id=1, source_target_pairs={{0,256},{256,0},{1,257},{257,1},{2,258},{258,2},{3,259},{259,3},{4... | collective-permute-start | bytes 196616 | tf_op jit(solution)/shard_map/ppermute | solution.py:236
  94.0 0.0 copy-done.3
  94.0 0.4 near_sum.1
  94.4 3.8 %collective-permute-done = bf16[256,128]{1,0:T(8,128)(2,1)S(1)} collective-permute-done((bf16[256,128]{1,0:T(8,128)(2,1)S(1)}, bf16[256,128]{1,0:T(8,128)(2,1)S(1)}, u32[]{:S(2)}, u32[]{:S(2)}) %collective-permute-start) | collective-permute-done | bytes 65568 | tf_op jit(solution)/shard_map/ppermute | solution.py:236
  98.2 0.7 convert_add_fusion
Async XLA Ops:
  0.0 56.9 %copy-start.1 = (bf16[256,256]{1,0:T(8,128)(2,1)S(1)}, bf16[256,256]{1,0:T(8,128)(2,1)}, u32[]{:S(2)}) copy-start(bf16[256,256]{1,0:T(8,128)(2,1)} %w2_ref.1) | copy-start | bytes 393220
  0.0 56.9 %copy-start.2 = (f32[256]{0:T(256)S(1)}, f32[256]{0:T(256)}, u32[]{:S(2)}) copy-start(f32[256]{0:T(256)} %param.15) | copy-start | bytes 3076
  0.0 56.9 %copy-start = (bf16[256,256]{1,0:T(8,128)(2,1)S(1)}, bf16[256,256]{1,0:T(8,128)(2,1)}, u32[]{:S(2)}) copy-start(bf16[256,256]{1,0:T(8,128)(2,1)} %w1_ref.1) | copy-start | bytes 393220
  27.1 66.9 %copy-start.3 = (f32[256]{0:T(256)S(1)}, f32[256]{0:T(256)}, u32[]{:S(2)}) copy-start(f32[256]{0:T(256)} %param.17) | copy-start | bytes 3076
  86.7 11.5 %collective-permute-start = (bf16[256,128]{1,0:T(8,128)(2,1)S(1)}, bf16[256,128]{1,0:T(8,128)(2,1)S(1)}, u32[]{:S(2)}, u32[]{:S(2)}) collective-permute-start(bf16[256,128]{1,0:T(8,128)(2,1)S(1)} %far_sum.1), channel_id=1, source_target_pairs={{0,256},{256,0},{1,257},{257,1},{2,258},{258,2},{3,259},{259,3},{4... | collective-permute-start | bytes 196616 | tf_op jit(solution)/shard_map/ppermute | solution.py:236
